TPU v7x, 32 devices: a whole 2x2x4 slice. The times are simulated.
32 devices in a mesh: grp: 1, dev: 16 (over z, y, core), section: 2 (over x), tp: 1.
Axes of the slice: x: 2, y: 2, z: 4, core: 2. Of those that a mesh axis runs over, the one named last changes fastest.
Arguments:
- prompt_pages: bfloat16 [32, 32, 16, 576], P(('grp', 'dev', 'section', 'tp')), may hold values from -6 to 6
- send_page: int32 [32, 32], P(('grp', 'dev', 'section', 'tp')), may hold values from -1 to 31, as said below
- page_table: int32 [32, 2, 16], P(('grp', 'dev', 'section', 'tp')), may hold values from -1 to 31, as said below
- context_len: int32 [32, 2], P(('grp', 'dev', 'section', 'tp')), may hold values from 1 to 256, as said below
- new_latent: bfloat16 [32, 2, 4, 576], P(('grp', 'dev', 'section', 'tp')), may hold values from -8 to 8
- queries: bfloat16 [32, 2, 4, 64, 576], P(('grp', 'dev', 'section', 'tp')), may hold values from -120 to 120
- moe_rows: bfloat16 [32, 4, 3584], P(('grp', 'dev', 'section', 'tp')), may hold values from -6 to 6
- routing: int32 [32, 4, 8], P(('grp', 'dev', 'section', 'tp')), may hold values from 0 to 15, all different within a row; in each aligned block of 4 rows (0 to 3, 4 to 7, ..., all dimensions but the last counted through in order) at most 3 rows name the same one
- gate_weights: float32 [32, 4, 8], P(('grp', 'dev', 'section', 'tp')), may hold values from 0.05 to 0.5
- expert_gate: bfloat16 [16, 3584, 1024], P('dev', None, ('section', 'tp')), may hold values from -0.09375 to 0.09375
- expert_up: bfloat16 [16, 3584, 1024], P('dev', None, ('section', 'tp')), may hold values from -0.09375 to 0.09375
- expert_down: bfloat16 [16, 1024, 3584], P('dev', ('section', 'tp')), may hold values from -0.1875 to 0.1875
Outputs:
- attended: bfloat16 [32, 2, 4, 64, 512], P(('grp', 'dev', 'section', 'tp'))
- expert_out: bfloat16 [32, 4, 3584], P(('grp', 'dev', 'section', 'tp'))
Inputs may be any that keep to these rules, and one draw needn't show every extreme that they name: context_len of some request of every rank is exactly 256. `page_table`: of a rank's entries, those with p < ceil(context_len / 16) are distinct slots, all others -1. `send_page`: an outgoing slot holds a page exactly when the receiving rank's page_table names it; the pages of one rank named are distinct. `routing`: no rank names one expert in more than 3 of its assignments.
All inputs are finite; a program needn't handle non-finite values.
Results may differ from a plain program's by a relative error of at most 0.02.
Values may be sent and summed in bfloat16 or wider, within the bound.
No kernel may reach another device: no remote copies, remote signals or barrier semaphores. Data moves between devices by JAX's collectives and lax.ppermute only.
A program may use at most 64 MiB of HBM per device.

v0:
```python
import jax
import jax.numpy as jnp
from jax import lax
from jax.experimental import pallas as pl
from jax.experimental.pallas import tpu as pltpu
from jax.sharding import PartitionSpec as P

VDIM = 512
SCALE = 192.0 ** (-0.5)
RANK = ("dev", "section", "tp")
VMEM_LIMIT = 50 * 1024 * 1024


def levels_of(peers, blocks):
    low = blocks.bit_length() - 1
    bits = peers.bit_length() - 1
    far = [low + bit for bit in range(2, bits)]
    near = list(range(low)) + [low + bit for bit in range(1, min(bits, 2))]
    last = [low + bit for bit in range(min(bits, 1))]
    return far, near, last


def masks_of(bits):
    masks = [0]
    for bit in bits:
        masks += [mask | (1 << bit) for mask in masks]
    return masks


def exchange(value, mask):
    count = lax.axis_size(RANK)
    return lax.ppermute(value, RANK, [(at, at ^ mask) for at in range(count)])


def pairs_of(bits):
    return [bits[at : at + 2] for at in range(0, len(bits), 2)]


def collect(value, bits):
    masks = masks_of(bits)
    count = value.shape[0] // len(masks)
    total = value[:count].astype(jnp.float32)
    for turn in range(1, len(masks)):
        sent = value[turn * count : (turn + 1) * count]
        total = total + exchange(sent, masks[turn]).astype(jnp.float32)
    return total.astype(jnp.bfloat16)


def experts_kernel(
    first_ref, own_ref, got_ref, gate_hbm, up_hbm, down_hbm, kept_ref, sent_ref,
    rows_ref, hidden_ref, gate_ref, up_ref, down_ref, in_sem, down_sem,
):
    count = own_ref.shape[0]
    owned, width, units = gate_hbm.shape
    experts = first_ref[1]
    step = min(units, 256)
    wide = 512 if width % 512 == 0 else 128
    turns, ends = units // step, width // wide

    def load_in(which, own, turn):
        source, target = ((gate_hbm, gate_ref), (up_hbm, up_ref))[which]
        part = (own, slice(None), pl.ds(turn * step, step))
        return pltpu.make_async_copy(source.at[part], target.at[part], in_sem.at[which, own, turn])

    def load_down(own, turn):
        part = (own, slice(None), pl.ds(turn * wide, wide))
        return pltpu.make_async_copy(down_hbm.at[part], down_ref.at[part], down_sem.at[own, turn])

    for own in range(owned):
        for turn in range(turns):
            load_in(0, own, turn).start()
            load_in(1, own, turn).start()
    for turn in range(ends):
        for own in range(owned):
            load_down(own, turn).start()
    rows_ref[:count] = own_ref[...]
    rows_ref[count:] = got_ref[...]
    extra = rows_ref[:, width:].astype(jnp.float32)
    lane = lax.broadcasted_iota(jnp.int32, extra.shape, 1)
    weights = []
    for own in range(owned):
        expert = first_ref[0] + own
        named = (lane == expert) | (lane == expert + experts)
        weights.append(jnp.sum(jnp.where(named, extra, 0.0), axis=1, keepdims=True))
        for turn in range(turns):
            part = pl.ds(turn * step, step)
            x = rows_ref[:, :width]
            load_in(0, own, turn).wait()
            gate = jnp.dot(x, gate_ref[own, :, part], preferred_element_type=jnp.float32)
            load_in(1, own, turn).wait()
            up = jnp.dot(x, up_ref[own, :, part], preferred_element_type=jnp.float32)
            hidden = gate / (1.0 + jnp.exp(-gate)) * up
            hidden_ref[own, :, part] = hidden.astype(jnp.bfloat16)
    for turn in range(ends):
        part = pl.ds(turn * wide, wide)
        total = None
        for own in range(owned):
            load_down(own, turn).wait()
            term = jnp.dot(
                hidden_ref[own], down_ref[own, :, part], preferred_element_type=jnp.float32
            ) * weights[own]
            total = term if total is None else total + term
        total = total.astype(jnp.bfloat16)
        kept_ref[:, part] = total[:count]
        sent_ref[:, part] = total[count:]


def experts_of(own, got, first, experts, expert_gate, expert_up, expert_down):
    count, packed = own.shape
    owned, width, units = expert_gate.shape
    scalars = jnp.stack([first, jnp.int32(experts)])
    vmem = pl.BlockSpec(memory_space=pltpu.VMEM)
    hbm = pl.BlockSpec(memory_space=pltpu.HBM)
    half = jax.ShapeDtypeStruct((count, width), jnp.bfloat16)
    step = min(units, 256)
    wide = 512 if width % 512 == 0 else 128
    return pl.pallas_call(
        experts_kernel,
        out_shape=(half, half),
        in_specs=[pl.BlockSpec(memory_space=pltpu.SMEM), vmem, vmem, hbm, hbm, hbm],
        out_specs=(vmem, vmem),
        scratch_shapes=[
            pltpu.VMEM((2 * count, packed), jnp.bfloat16),
            pltpu.VMEM((owned, 2 * count, units), jnp.bfloat16),
            pltpu.VMEM(expert_gate.shape, jnp.bfloat16),
            pltpu.VMEM(expert_up.shape, jnp.bfloat16),
            pltpu.VMEM(expert_down.shape, jnp.bfloat16),
            pltpu.SemaphoreType.DMA((2, owned, units // step)),
            pltpu.SemaphoreType.DMA((owned, width // wide)),
        ],
        compiler_params=pltpu.CompilerParams(vmem_limit_bytes=VMEM_LIMIT),
        cost_estimate=pl.CostEstimate(
            flops=120 * count * owned * width * units,
            bytes_accessed=6 * owned * width * units,
            transcendentals=2 * count * owned * units,
        ),
        name="experts",
    )(scalars, own, got, expert_gate, expert_up, expert_down)


def attend(queries, new_latent, cache, lengths):
    steps = queries.shape[1]
    ctx = cache.shape[1]
    keys = jnp.concatenate([cache, new_latent], axis=1)
    scores = jnp.einsum("rshl,rkl->rshk", queries, keys, preferred_element_type=jnp.float32) * SCALE
    position = jnp.arange(ctx + steps)
    step_index = jnp.arange(steps)
    in_cache = position[None, :] < lengths[:, None]
    in_new = (position[None, :] >= ctx) & (position[None, :] - ctx <= step_index[:, None])
    allowed = in_cache[:, None, :] | in_new[None, :, :]
    scores = jnp.where(allowed[:, :, None, :], scores, -jnp.inf)
    top = jnp.max(scores, axis=-1, keepdims=True)
    weights = jnp.exp(scores - top)
    weights = (weights / jnp.sum(weights, axis=-1, keepdims=True)).astype(jnp.bfloat16)
    values = keys[:, :, :VDIM]
    return jnp.einsum("rshk,rkv->rshv", weights, values, preferred_element_type=jnp.float32).astype(
        jnp.bfloat16
    )


def body(
    prompt_pages,
    send_page,
    page_table,
    context_len,
    new_latent,
    queries,
    moe_rows,
    routing,
    gate_weights,
    expert_gate,
    expert_up,
    expert_down,
):
    peers = lax.axis_size("dev")
    pages = prompt_pages[0]
    outgoing_slots = send_page[0]
    page_len, width_lat = (pages.shape[1], pages.shape[2])
    capp = outgoing_slots.shape[0] // peers
    picked_pages = pages[jnp.maximum(outgoing_slots, 0)]
    arrived = lax.all_to_all(
        picked_pages.reshape(peers, capp, page_len, width_lat),
        "dev",
        split_axis=0,
        concat_axis=0,
        tiled=True,
    )
    arrived = arrived.reshape(peers * capp, page_len, width_lat)

    owned = expert_gate.shape[0]
    experts = peers * owned
    rows = routing.shape[1]
    width = moe_rows.shape[2]
    named = routing[0][:, :, None] == jnp.arange(experts)[None, None, :]
    dense = jnp.sum(jnp.where(named, gate_weights[0][:, :, None], 0.0), axis=1)
    high = dense.astype(jnp.bfloat16)
    low = (dense - high.astype(jnp.float32)).astype(jnp.bfloat16)
    extra = jnp.concatenate([high, low], axis=1)
    pad = -extra.shape[1] % 128
    packed = jnp.concatenate([moe_rows[0], jnp.pad(extra, ((0, 0), (0, pad)))], axis=1)
    far, near, last = levels_of(peers, lax.axis_size(("section", "tp")))
    pooled = packed
    for bits in pairs_of(far):
        pooled = jnp.concatenate([pooled] + [exchange(pooled, mask) for mask in masks_of(bits)[1:]], axis=0)
    pooled = jnp.concatenate([pooled] + [exchange(pooled, mask) for mask in masks_of(near)[1:]], axis=0)
    other = masks_of(last)[-1]
    first = lax.axis_index("dev") * owned
    kept, sent = experts_of(
        pooled, exchange(pooled, other), first, experts, expert_gate, expert_up, expert_down
    )
    mixed = kept.astype(jnp.float32) + exchange(sent, other).astype(jnp.float32)
    mixed = mixed.astype(jnp.bfloat16)
    for bits in [near] + pairs_of(far)[::-1]:
        mixed = collect(mixed, bits)

    table = page_table[0]
    requests, most_pages = table.shape
    cache = arrived[jnp.maximum(table, 0)].reshape(requests, most_pages * page_len, width_lat)
    attended = attend(queries[0], new_latent[0], cache, context_len[0])
    return (attended[None], mixed[None])


def solution(mesh):
    rank = ("grp",) + RANK
    return jax.shard_map(
        body,
        mesh=mesh,
        in_specs=(
            P(rank, None, None, None),
            P(rank, None),
            P(rank, None, None),
            P(rank, None),
            P(rank, None, None, None),
            P(rank, None, None, None, None),
            P(rank, None, None),
            P(rank, None, None),
            P(rank, None, None),
            P("dev", None, ("section", "tp")),
            P("dev", None, ("section", "tp")),
            P("dev", ("section", "tp"), None),
        ),
        out_specs=(
            P(rank, None, None, None, None),
            P(rank, None, None),
        ),
        check_vma=False,
    )
```

profile of v0, /device:TPU:0, one launch (start us, length us, event | category | flops | bytes accessed | tf_op | source)
XLA Modules:
  0.0 60.3 jit_solution(3867906139609725674)
XLA Ops:
  0.6 0.8 %select_reduce_fusion = f32[4,16]{1,0:T(4,128)S(1)} fusion(f32[4,8]{1,0:T(4,128)} %bitcast.53, s32[4,8]{1,0:T(4,128)} %bitcast.54), kind=kLoop, calls=%fused_computation.26 | loop fusion | flops 1472 | bytes 512 | tf_op jit(solution)/shard_map/reduce_sum | solution.py:195
  1.6 0.8 %pad_maximum_fusion.2 = bf16[4,3712]{1,0:T(4,128)(2,1)S(1)} fusion(bf16[4,128]{1,0:T(4,128)(2,1)S(1)} %fusion.22, bf16[4,3584]{1,0:T(4,128)(2,1)} %bitcast.51), kind=kLoop, calls=%fused_computation.24 | loop fusion | flops 59392 | bytes 59392 | tf_op jit(solution)/shard_map/concatenate | solution.py:200
  2.4 5.1 %collective-permute-start.2 = (bf16[4,3712]{1,0:T(4,128)(2,1)S(1)}, bf16[4,3712]{1,0:T(4,128)(2,1)S(1)}, u32[]{:S(2)}, u32[]{:S(2)}) collective-permute-start(bf16[4,3712]{1,0:T(4,128)(2,1)S(1)} %pad_maximum_fusion.2), channel_id=1, source_target_pairs={{0,24},{1,25},{2,26},{3,27},{4,28},{5,29},{6,30},{7,31},{8,16},{9,... | collective-permute-start | bytes 89096 | tf_op jit(solution)/shard_map/ppermute | solution.py:32
  7.5 0.6 %collective-permute-start = (bf16[4,3712]{1,0:T(4,128)(2,1)S(1)}, bf16[4,3712]{1,0:T(4,128)(2,1)S(1)}, u32[]{:S(2)}, u32[]{:S(2)}) collective-permute-start(bf16[4,3712]{1,0:T(4,128)(2,1)S(1)} %pad_maximum_fusion.2), channel_id=1, source_target_pairs={{0,8},{1,9},{2,10},{3,11},{4,12},{5,13},{6,14},{7,15},{8,0},{9,1},... | collective-permute-start | bytes 89096 | tf_op jit(solution)/shard_map/ppermute | solution.py:32
  8.1 0.7 %maximum_bitcast_fusion = s32[32]{0:T(128)S(1)} fusion(s32[1,32]{1,0:T(1,128)} %param.13), kind=kLoop, calls=%fused_computation.43 | loop fusion | flops 32 | bytes 256 | tf_op jit(solution)/shard_map/max | solution.py:180
  8.8 1.5 %gather_fusion = bf16[32,16,576]{2,1,0:T(8,128)(2,1)} fusion(bf16[32,16,576]{2,1,0:T(8,128)(2,1)S(1)} %bitcast.46, s32[1024]{0:T(1024)S(1)} %pad_clamp_fusion.1), kind=kCustom, calls=%fused_computation | custom fusion | bytes 1179776 | tf_op jit(solution)/shard_map/gather | solution.py:180
  10.3 6.2 %all-to-all-start = ((bf16[16,2,16,576]{3,2,1,0:T(8,128)(2,1)}), bf16[16,2,16,576]{3,2,1,0:T(8,128)(2,1)S(1)}, u32[]{:S(2)}, u32[]{:S(2)}) async-start(bf16[16,2,16,576]{3,2,1,0:T(8,128)(2,1)} %bitcast.3), calls=%async_computation | async-start | bytes 1310720 | tf_op jit(solution)/shard_map/all_to_all | solution.py:181
  16.6 2.9 %collective-permute-start.5 = (bf16[16,3712]{1,0:T(8,128)(2,1)S(1)}, bf16[16,3712]{1,0:T(8,128)(2,1)S(1)}, u32[]{:S(2)}, u32[]{:S(2)}) collective-permute-start(bf16[16,3712]{1,0:T(8,128)(2,1)S(1)} %pad_maximum_fusion.1), channel_id=1, source_target_pairs={{0,5},{1,4},{2,7},{3,6},{4,1},{5,0},{6,3},{7,2},{8,13},{9,12},{10,... | collective-permute-start | bytes 356360 | tf_op jit(solution)/shard_map/ppermute | solution.py:32
  19.5 0.1 collective-permute-start.4
  19.6 0.5 collective-permute-start.3
  20.2 5.1 %collective-permute-done.5 = bf16[16,3712]{1,0:T(8,128)(2,1)S(1)} collective-permute-done((bf16[16,3712]{1,0:T(8,128)(2,1)S(1)}, bf16[16,3712]{1,0:T(8,128)(2,1)S(1)}, u32[]{:S(2)}, u32[]{:S(2)}) %collective-permute-start.5) | collective-permute-done | bytes 118816 | tf_op jit(solution)/shard_map/ppermute | solution.py:32
  25.2 4.7 %collective-permute-done.4 = bf16[16,3712]{1,0:T(8,128)(2,1)S(1)} collective-permute-done((bf16[16,3712]{1,0:T(8,128)(2,1)S(1)}, bf16[16,3712]{1,0:T(8,128)(2,1)S(1)}, u32[]{:S(2)}, u32[]{:S(2)}) %collective-permute-start.4) | collective-permute-done | bytes 118816 | tf_op jit(solution)/shard_map/ppermute | solution.py:32
  30.0 0.2 concatenate.20.own_ref
  30.5 1.6 %collective-permute-done.6.got_ref = bf16[64,3712]{1,0:T(8,128)(2,1)S(1)} collective-permute-done((bf16[64,3712]{1,0:T(8,128)(2,1)S(1)}, bf16[64,3712]{1,0:T(8,128)(2,1)S(1)}, u32[]{:S(2)}, u32[]{:S(2)}) %collective-permute-start.6) | collective-permute-done | bytes 475168 | tf_op jit(solution)/shard_map/ppermute | solution.py:32
  32.1 7.0 %experts.1 = (bf16[64,3584]{1,0:T(8,128)(2,1)S(1)}, bf16[64,3584]{1,0:T(8,128)(2,1)S(1)}) custom-call(s32[2]{0:T(128)S(1)} %pad_add_fusion.first_ref, bf16[64,3712]{1,0:T(8,128)(2,1)S(1)} %concatenate.20.own_ref, bf16[64,3712]{1,0:T(8,128)(2,1)S(1)} %collective-permute-done.6.got_ref, bf16[1,3584,512]{2,1,0:T(8,128)(2,1)} %gate_hbm.1, ...), custom_call_target="tpu_custom_call" | custom-call | flops 14092861440 | bytes 11010048 | tf_op jit(solution)/shard_map/experts/pallas_call | solution.py:117
  39.1 0.2 collective-permute-start.7
  39.3 1.6 %collective-permute-done.7 = bf16[64,3584]{1,0:T(8,128)(2,1)S(1)} collective-permute-done((bf16[64,3584]{1,0:T(8,128)(2,1)S(1)}, bf16[64,3584]{1,0:T(8,128)(2,1)S(1)}, u32[]{:S(2)}, u32[]{:S(2)}) %collective-permute-start.7) | collective-permute-done | bytes 458784 | tf_op jit(solution)/shard_map/ppermute | solution.py:32
  41.0 0.1 add_convert_fusion
  41.1 1.6 %collective-permute-start.8 = (bf16[16,3584]{1,0:T(8,128)(2,1)S(1)}, bf16[16,3584]{1,0:T(8,128)(2,1)S(1)}, u32[]{:S(2)}, u32[]{:S(2)}) collective-permute-start(bf16[16,3584]{1,0:T(8,128)(2,1)S(1)} %get-tuple-element.8), channel_id=1, source_target_pairs={{0,1},{1,0},{2,3},{3,2},{4,5},{5,4},{6,7},{7,6},{8,9},{9,8},{10,11... | collective-permute-start | bytes 344072 | tf_op jit(solution)/shard_map/ppermute | solution.py:32
  42.7 1.4 %collective-permute-start.10 = (bf16[16,3584]{1,0:T(8,128)(2,1)S(1)}, bf16[16,3584]{1,0:T(8,128)(2,1)S(1)}, u32[]{:S(2)}, u32[]{:S(2)}) collective-permute-start(bf16[16,3584]{1,0:T(8,128)(2,1)S(1)} %get-tuple-element.9), channel_id=1, source_target_pairs={{0,5},{1,4},{2,7},{3,6},{4,1},{5,0},{6,3},{7,2},{8,13},{9,12},{10,... | collective-permute-start | bytes 344072 | tf_op jit(solution)/shard_map/ppermute | solution.py:32
  44.1 0.6 collective-permute-start.9
  44.7 0.7 %gather_fusion.1 = bf16[32,16,576]{2,1,0:T(8,128)(2,1)S(1)} fusion(bf16[32,16,576]{2,1,0:T(8,128)(2,1)S(1)} %bitcast.47, s32[1024]{0:T(1024)S(1)} %pad_clamp_fusion), kind=kCustom, calls=%fused_computation.1 | custom fusion | bytes 1179776 | tf_op jit(solution)/shard_map/gather | solution.py:218
  45.4 2.6 %fusion.4 = f32[2,4,64,260]{3,2,1,0:T(8,128)} fusion(bf16[2,4,576]{2,1,0:T(4,128)(2,1)S(1)} %bitcast.56, bf16[1,2,4,64,576]{4,3,2,1,0:T(8,128)(2,1)} %param.17, bf16[2,256,576]{2,1,0:T(8,128)(2,1)S(1)} %bitcast.48, pred[2,4,260]{2,1,0:T(4,128)(4,1)S(1)} %broadcast_or_fusion), kind=kOutput, calls=%fused_computation.8 | convolution fusion | flops 154818560 | bytes 1723424 | tf_op jit(solution)/shard_map/rshl,rkl->rshk/dot_general | solution.py:145
  48.0 0.8 %fusion.32 = f32[2,4,64]{2,1,0:T(4,128)S(1)} fusion(bf16[2,4,576]{2,1,0:T(4,128)(2,1)S(1)} %bitcast.57, bf16[1,2,4,64,576]{4,3,2,1,0:T(8,128)(2,1)S(1)} %copy-done.4, bf16[2,256,576]{2,1,0:T(8,128)(2,1)S(1)} %bitcast.49, pred[2,4,260]{2,1,0:T(4,128)(4,1)S(1)} %broadcast_or_fusion), kind=kOutput, calls=%fused_computation.52 | convolution fusion | flops 155085056 | bytes 1192992 | tf_op jit(solution)/shard_map/sub | solution.py:153
  48.8 1.1 %collective-permute-done.10 = bf16[16,3584]{1,0:T(8,128)(2,1)S(1)} collective-permute-done((bf16[16,3584]{1,0:T(8,128)(2,1)S(1)}, bf16[16,3584]{1,0:T(8,128)(2,1)S(1)}, u32[]{:S(2)}, u32[]{:S(2)}) %collective-permute-start.10) | collective-permute-done | bytes 114720 | tf_op jit(solution)/shard_map/ppermute | solution.py:32
  49.8 1.4 %collective-permute-done.9 = bf16[16,3584]{1,0:T(8,128)(2,1)S(1)} collective-permute-done((bf16[16,3584]{1,0:T(8,128)(2,1)S(1)}, bf16[16,3584]{1,0:T(8,128)(2,1)S(1)}, u32[]{:S(2)}, u32[]{:S(2)}) %collective-permute-start.9) | collective-permute-done | bytes 114720 | tf_op jit(solution)/shard_map/ppermute | solution.py:32
  51.3 1.3 %collective-permute-start.11 = (bf16[4,3584]{1,0:T(4,128)(2,1)S(1)}, bf16[4,3584]{1,0:T(4,128)(2,1)S(1)}, u32[]{:S(2)}, u32[]{:S(2)}) collective-permute-start(bf16[4,3584]{1,0:T(4,128)(2,1)S(1)} %get-tuple-element.11), channel_id=1, source_target_pairs={{0,8},{1,9},{2,10},{3,11},{4,12},{5,13},{6,14},{7,15},{8,0},{9,1},... | collective-permute-start | bytes 86024 | tf_op jit(solution)/shard_map/ppermute | solution.py:32
  52.6 2.4 %collective-permute-start.13 = (bf16[4,3584]{1,0:T(4,128)(2,1)S(1)}, bf16[4,3584]{1,0:T(4,128)(2,1)S(1)}, u32[]{:S(2)}, u32[]{:S(2)}) collective-permute-start(bf16[4,3584]{1,0:T(4,128)(2,1)S(1)} %get-tuple-element.12), channel_id=1, source_target_pairs={{0,24},{1,25},{2,26},{3,27},{4,28},{5,29},{6,30},{7,31},{8,16},{9,... | collective-permute-start | bytes 86024 | tf_op jit(solution)/shard_map/ppermute | solution.py:32
  54.9 0.3 collective-permute-start.12
  55.2 3.3 %fusion.5 = bf16[1,2,4,64,512]{4,3,2,1,0:T(8,128)(2,1)} fusion(bf16[2,256,576]{2,1,0:T(8,128)(2,1)S(1)} %bitcast.50, bf16[2,4,576]{2,1,0:T(4,128)(2,1)S(1)} %bitcast.58, f32[2,4,64]{2,1,0:T(4,128)S(1)} %fusion.32, f32[2,4,64,260]{3,2,1,0:T(8,128)} %fusion.4), kind=kOutput, calls=%fused_computation.9 | convolution fusion | flops 138042112 | bytes 2698240 | tf_op jit(solution)/shard_map/rshk,rkv->rshv/dot_general | solution.py:156
  58.5 1.2 %collective-permute-done.12 = bf16[4,3584]{1,0:T(4,128)(2,1)S(1)} collective-permute-done((bf16[4,3584]{1,0:T(4,128)(2,1)S(1)}, bf16[4,3584]{1,0:T(4,128)(2,1)S(1)}, u32[]{:S(2)}, u32[]{:S(2)}) %collective-permute-start.12) | collective-permute-done | bytes 28704 | tf_op jit(solution)/shard_map/ppermute | solution.py:32
  59.7 0.6 %fusion.14 = bf16[1,4,3584]{2,1,0:T(4,128)(2,1)} fusion(bf16[4,3584]{1,0:T(4,128)(2,1)S(1)} %collective-permute-done.13, bf16[4,3584]{1,0:T(4,128)(2,1)S(1)} %collective-permute-done.12, bf16[4,3584]{1,0:T(4,128)(2,1)S(1)} %collective-permute-done.11, bf16[16,3584]{1,0:T(8,128)(2,1)S(1)} %add_convert_fusion.1), kind=kLoop, calls=%fused_computation.25 | loop fusion | flops 114688 | bytes 143360 | tf_op jit(solution)/shard_map/broadcast_in_dim | solution.py:220
  (38 shorter events, 0.7 us)
Async XLA Ops:
  0.6 8.2 %copy-start = (bf16[1,32,16,576]{3,2,1,0:T(8,128)(2,1)S(1)}, bf16[1,32,16,576]{3,2,1,0:T(8,128)(2,1)}, u32[]{:S(2)}) copy-start(bf16[1,32,16,576]{3,2,1,0:T(8,128)(2,1)} %param.12) | copy-start | bytes 1769476
  1.5 15.0 %copy-start.1 = (bf16[1,4,3584]{2,1,0:T(4,128)(2,1)S(1)}, bf16[1,4,3584]{2,1,0:T(4,128)(2,1)}, u32[]{:S(2)}) copy-start(bf16[1,4,3584]{2,1,0:T(4,128)(2,1)} %param.18) | copy-start | bytes 86020
  2.4 14.1 %collective-permute-start.2 = (bf16[4,3712]{1,0:T(4,128)(2,1)S(1)}, bf16[4,3712]{1,0:T(4,128)(2,1)S(1)}, u32[]{:S(2)}, u32[]{:S(2)}) collective-permute-start(bf16[4,3712]{1,0:T(4,128)(2,1)S(1)} %pad_maximum_fusion.2), channel_id=1, source_target_pairs={{0,24},{1,25},{2,26},{3,27},{4,28},{5,29},{6,30},{7,31},{8,16},{9,... | collective-permute-start | bytes 89096 | tf_op jit(solution)/shard_map/ppermute | solution.py:32
  7.5 9.0 %collective-permute-start.1 = (bf16[4,3712]{1,0:T(4,128)(2,1)S(1)}, bf16[4,3712]{1,0:T(4,128)(2,1)S(1)}, u32[]{:S(2)}, u32[]{:S(2)}) collective-permute-start(bf16[4,3712]{1,0:T(4,128)(2,1)S(1)} %pad_maximum_fusion.2), channel_id=1, source_target_pairs={{0,16},{1,17},{2,18},{3,19},{4,20},{5,21},{6,22},{7,23},{8,24},{9,... | collective-permute-start | bytes 89096 | tf_op jit(solution)/shard_map/ppermute | solution.py:32
  7.5 9.0 %collective-permute-start = (bf16[4,3712]{1,0:T(4,128)(2,1)S(1)}, bf16[4,3712]{1,0:T(4,128)(2,1)S(1)}, u32[]{:S(2)}, u32[]{:S(2)}) collective-permute-start(bf16[4,3712]{1,0:T(4,128)(2,1)S(1)} %pad_maximum_fusion.2), channel_id=1, source_target_pairs={{0,8},{1,9},{2,10},{3,11},{4,12},{5,13},{6,14},{7,15},{8,0},{9,1},... | collective-permute-start | bytes 89096 | tf_op jit(solution)/shard_map/ppermute | solution.py:32
  8.8 11.4 %copy-start.2 = (s32[1,2,16]{2,1,0:T(2,128)S(1)}, s32[1,2,16]{2,1,0:T(2,128)}, u32[]{:S(2)}) copy-start(s32[1,2,16]{2,1,0:T(2,128)} %param.14) | copy-start | bytes 388
  10.3 20.1 %copy-start.3 = (s32[1,2]{1,0:T(1,128)S(1)}, s32[1,2]{1,0:T(1,128)}, u32[]{:S(2)}) copy-start(s32[1,2]{1,0:T(1,128)} %param.15) | copy-start | bytes 28
  10.3 34.4 %all-to-all-start = ((bf16[16,2,16,576]{3,2,1,0:T(8,128)(2,1)}), bf16[16,2,16,576]{3,2,1,0:T(8,128)(2,1)S(1)}, u32[]{:S(2)}, u32[]{:S(2)}) async-start(bf16[16,2,16,576]{3,2,1,0:T(8,128)(2,1)} %bitcast.3), calls=%async_computation | async-start | bytes 1310720 | tf_op jit(solution)/shard_map/all_to_all | solution.py:181
  16.6 8.6 %collective-permute-start.5 = (bf16[16,3712]{1,0:T(8,128)(2,1)S(1)}, bf16[16,3712]{1,0:T(8,128)(2,1)S(1)}, u32[]{:S(2)}, u32[]{:S(2)}) collective-permute-start(bf16[16,3712]{1,0:T(8,128)(2,1)S(1)} %pad_maximum_fusion.1), channel_id=1, source_target_pairs={{0,5},{1,4},{2,7},{3,6},{4,1},{5,0},{6,3},{7,2},{8,13},{9,12},{10,... | collective-permute-start | bytes 356360 | tf_op jit(solution)/shard_map/ppermute | solution.py:32
  19.5 10.4 %collective-permute-start.4 = (bf16[16,3712]{1,0:T(8,128)(2,1)S(1)}, bf16[16,3712]{1,0:T(8,128)(2,1)S(1)}, u32[]{:S(2)}, u32[]{:S(2)}) collective-permute-start(bf16[16,3712]{1,0:T(8,128)(2,1)S(1)} %pad_maximum_fusion.1), channel_id=1, source_target_pairs={{0,4},{1,5},{2,6},{3,7},{4,0},{5,1},{6,2},{7,3},{8,12},{9,13},{10,... | collective-permute-start | bytes 356360 | tf_op jit(solution)/shard_map/ppermute | solution.py:32
  19.6 10.3 %collective-permute-start.3 = (bf16[16,3712]{1,0:T(8,128)(2,1)S(1)}, bf16[16,3712]{1,0:T(8,128)(2,1)S(1)}, u32[]{:S(2)}, u32[]{:S(2)}) collective-permute-start(bf16[16,3712]{1,0:T(8,128)(2,1)S(1)} %pad_maximum_fusion.1), channel_id=1, source_target_pairs={{0,1},{1,0},{2,3},{3,2},{4,5},{5,4},{6,7},{7,6},{8,9},{9,8},{10,11... | collective-permute-start | bytes 356360 | tf_op jit(solution)/shard_map/ppermute | solution.py:32
  30.2 1.9 %collective-permute-start.6 = (bf16[64,3712]{1,0:T(8,128)(2,1)S(1)}, bf16[64,3712]{1,0:T(8,128)(2,1)S(1)}, u32[]{:S(2)}, u32[]{:S(2)}) collective-permute-start(bf16[64,3712]{1,0:T(8,128)(2,1)S(1)} %concatenate.20.own_ref), channel_id=1, source_target_pairs={{0,2},{1,3},{2,0},{3,1},{4,6},{5,7},{6,4},{7,5},{8,10},{9,11},{10,... | collective-permute-start | bytes 1425416 | tf_op jit(solution)/shard_map/ppermute | solution.py:32
  39.1 1.9 %collective-permute-start.7 = (bf16[64,3584]{1,0:T(8,128)(2,1)S(1)}, bf16[64,3584]{1,0:T(8,128)(2,1)S(1)}, u32[]{:S(2)}, u32[]{:S(2)}) collective-permute-start(bf16[64,3584]{1,0:T(8,128)(2,1)S(1)} %get-tuple-element.5), channel_id=1, source_target_pairs={{0,2},{1,3},{2,0},{3,1},{4,6},{5,7},{6,4},{7,5},{8,10},{9,11},{10,... | collective-permute-start | bytes 1376264 | tf_op jit(solution)/shard_map/ppermute | solution.py:32
  41.0 4.4 %copy-start.5 = (bf16[1,2,4,576]{3,2,1,0:T(4,128)(2,1)S(1)}, bf16[1,2,4,576]{3,2,1,0:T(4,128)(2,1)}, u32[]{:S(2)}) copy-start(bf16[1,2,4,576]{3,2,1,0:T(4,128)(2,1)} %param.16) | copy-start | bytes 27652
  41.1 7.6 %collective-permute-start.8 = (bf16[16,3584]{1,0:T(8,128)(2,1)S(1)}, bf16[16,3584]{1,0:T(8,128)(2,1)S(1)}, u32[]{:S(2)}, u32[]{:S(2)}) collective-permute-start(bf16[16,3584]{1,0:T(8,128)(2,1)S(1)} %get-tuple-element.8), channel_id=1, source_target_pairs={{0,1},{1,0},{2,3},{3,2},{4,5},{5,4},{6,7},{7,6},{8,9},{9,8},{10,11... | collective-permute-start | bytes 344072 | tf_op jit(solution)/shard_map/ppermute | solution.py:32
  42.7 7.1 %collective-permute-start.10 = (bf16[16,3584]{1,0:T(8,128)(2,1)S(1)}, bf16[16,3584]{1,0:T(8,128)(2,1)S(1)}, u32[]{:S(2)}, u32[]{:S(2)}) collective-permute-start(bf16[16,3584]{1,0:T(8,128)(2,1)S(1)} %get-tuple-element.9), channel_id=1, source_target_pairs={{0,5},{1,4},{2,7},{3,6},{4,1},{5,0},{6,3},{7,2},{8,13},{9,12},{10,... | collective-permute-start | bytes 344072 | tf_op jit(solution)/shard_map/ppermute | solution.py:32
  44.1 7.1 %collective-permute-start.9 = (bf16[16,3584]{1,0:T(8,128)(2,1)S(1)}, bf16[16,3584]{1,0:T(8,128)(2,1)S(1)}, u32[]{:S(2)}, u32[]{:S(2)}) collective-permute-start(bf16[16,3584]{1,0:T(8,128)(2,1)S(1)} %get-tuple-element.10), channel_id=1, source_target_pairs={{0,4},{1,5},{2,6},{3,7},{4,0},{5,1},{6,2},{7,3},{8,12},{9,13},{10,... | collective-permute-start | bytes 344072 | tf_op jit(solution)/shard_map/ppermute | solution.py:32
  45.4 2.6 %copy-start.4 = (bf16[1,2,4,64,576]{4,3,2,1,0:T(8,128)(2,1)S(1)}, bf16[1,2,4,64,576]{4,3,2,1,0:T(8,128)(2,1)}, u32[]{:S(2)}) copy-start(bf16[1,2,4,64,576]{4,3,2,1,0:T(8,128)(2,1)} %param.17) | copy-start | bytes 1769476
  51.3 7.2 %collective-permute-start.11 = (bf16[4,3584]{1,0:T(4,128)(2,1)S(1)}, bf16[4,3584]{1,0:T(4,128)(2,1)S(1)}, u32[]{:S(2)}, u32[]{:S(2)}) collective-permute-start(bf16[4,3584]{1,0:T(4,128)(2,1)S(1)} %get-tuple-element.11), channel_id=1, source_target_pairs={{0,8},{1,9},{2,10},{3,11},{4,12},{5,13},{6,14},{7,15},{8,0},{9,1},... | collective-permute-start | bytes 86024 | tf_op jit(solution)/shard_map/ppermute | solution.py:32
  52.6 6.0 %collective-permute-start.13 = (bf16[4,3584]{1,0:T(4,128)(2,1)S(1)}, bf16[4,3584]{1,0:T(4,128)(2,1)S(1)}, u32[]{:S(2)}, u32[]{:S(2)}) collective-permute-start(bf16[4,3584]{1,0:T(4,128)(2,1)S(1)} %get-tuple-element.12), channel_id=1, source_target_pairs={{0,24},{1,25},{2,26},{3,27},{4,28},{5,29},{6,30},{7,31},{8,16},{9,... | collective-permute-start | bytes 86024 | tf_op jit(solution)/shard_map/ppermute | solution.py:32
  54.9 4.8 %collective-permute-start.12 = (bf16[4,3584]{1,0:T(4,128)(2,1)S(1)}, bf16[4,3584]{1,0:T(4,128)(2,1)S(1)}, u32[]{:S(2)}, u32[]{:S(2)}) collective-permute-start(bf16[4,3584]{1,0:T(4,128)(2,1)S(1)} %get-tuple-element.13), channel_id=1, source_target_pairs={{0,16},{1,17},{2,18},{3,19},{4,20},{5,21},{6,22},{7,23},{8,24},{9,... | collective-permute-start | bytes 86024 | tf_op jit(solution)/shard_map/ppermute | solution.py:32
where the time goes:
time: 60.7 us; the launch traced here: 60.3 us
  starting transfers between devices  23.3 us (38%)
  waiting for transfers between devices  16.6 us (27%)
  Pallas kernels  7.02 us (12%)
  matrix products  6.68 us (11%)
  other arithmetic  3.44 us (6%)
  local copies, waits for them, and re-layouts  2.5 us (4%)
  between operations  0.82 us (1%)
    ppermute x14, starting transfers between devices, exchange(): return lax.ppermute(value, RANK, [(at, at ^ mask) for at in range(count)])  17.1 us
    ppermute x14, waiting for transfers between devices, exchange(): return lax.ppermute(value, RANK, [(at, at ^ mask) for at in range(count)])  16.6 us
    pallas_call x1, Pallas kernels, experts_of(): pl.pallas_call(experts_kernel, out_shape=(half, half), in_specs=[pl.Block...  7.02 us
    all_to_all x1, starting transfers between devices, body(): lax.all_to_all(picked_pages.reshape(peers, capp, page_len, width_lat), 'd...  6.21 us
    dot_general x1, matrix products, attend(): jnp.einsum('rshk,rkv->rshv', weights, values, preferred_element_type=jnp....  3.31 us
    dot_general x1, matrix products, attend(): jnp.einsum('rshl,rkl->rshk', queries, keys, preferred_element_type=jnp.fl...  2.62 us
    gather x1, local copies, waits for them, and re-layouts, body(): picked_pages = pages[jnp.maximum(outgoing_slots, 0)]  1.48 us
  transfers between devices with their start and end apart: 15, of which 7 were waited for; matrix products, arithmetic and copies ran while one was open for 17% of the time, Pallas kernels for 12%

commit v1 on v0

--- a/solution.py
+++ b/solution.py
@@ -210,7 +210,9 @@
     )
     mixed = kept.astype(jnp.float32) + exchange(sent, other).astype(jnp.float32)
     mixed = mixed.astype(jnp.bfloat16)
-    for bits in [near] + pairs_of(far)[::-1]:
+    mixed = collect(mixed, near)
+    mixed, arrived = lax.optimization_barrier((mixed, arrived))
+    for bits in pairs_of(far)[::-1]:
         mixed = collect(mixed, bits)
 
     table = page_table[0]

time: 60.7 us -> 59.6 us (0.982)
  waiting for transfers between devices: 16.6 us -> 20.1 us
  matrix products: 6.68 us -> 3.24 us
  starting transfers between devices: 23.3 us -> 21.4 us
  other arithmetic: 3.44 us -> 4.18 us
    ppermute x14, waiting for transfers between devices: 16.6 us -> 20.1 us  [exchange(): return lax.ppermute(value, RANK, [(at, at ^ mask) for at in range(count)])]
    dot_general x1, matrix products: 2.62 us -> 0.56 us  [attend(): jnp.einsum('rshl,rkl->rshk', queries, keys, preferred_element_type=jnp.fl...]
    all_to_all x1, starting transfers between devices: 6.21 us -> 4.45 us  [body(): lax.all_to_all(picked_pages.reshape(peers, capp, page_len, width_lat), 'd...]
    dot_general x1, matrix products: 3.31 us -> 1.94 us  [attend(): jnp.einsum('rshk,rkv->rshv', weights, values, preferred_element_type=jnp....]
    concatenate x1, other arithmetic: 0.08 us -> 0.82 us  [body(): jnp.concatenate([pooled] + [exchange(pooled, mask) for mask in masks_of(b...]
  transfers between devices with their start and end apart: 15 -> 15, of which waited for: 7 -> 10; matrix products, arithmetic and copies ran while one was open for 17% -> 8% of each run, Pallas kernels for 12% -> 12%
where the time goes in v1:
time: 59.6 us; the launch traced here: 59.3 us
  starting transfers between devices  21.4 us (36%)
  waiting for transfers between devices  20.1 us (34%)
  Pallas kernels  7.02 us (12%)
  other arithmetic  4.18 us (7%)
  matrix products  3.24 us (5%)
  local copies, waits for them, and re-layouts  2.5 us (4%)
  between operations  0.81 us (1%)
    ppermute x14, waiting for transfers between devices, exchange(): return lax.ppermute(value, RANK, [(at, at ^ mask) for at in range(count)])  20.1 us
    ppermute x14, starting transfers between devices, exchange(): return lax.ppermute(value, RANK, [(at, at ^ mask) for at in range(count)])  17 us
    pallas_call x1, Pallas kernels, experts_of(): pl.pallas_call(experts_kernel, out_shape=(half, half), in_specs=[pl.Block...  7.02 us
    all_to_all x1, starting transfers between devices, body(): lax.all_to_all(picked_pages.reshape(peers, capp, page_len, width_lat), 'd...  4.45 us
    dot_general x1, matrix products, attend(): jnp.einsum('rshk,rkv->rshv', weights, values, preferred_element_type=jnp....  1.94 us
    gather x1, local copies, waits for them, and re-layouts, body(): picked_pages = pages[jnp.maximum(outgoing_slots, 0)]  1.48 us
  transfers between devices with their start and end apart: 15, of which 10 were waited for; matrix products, arithmetic and copies ran while one was open for 8% of the time, Pallas kernels for 12%

profile of v1, /device:TPU:0, one launch (start us, length us, event | category | flops | bytes accessed | tf_op | source)
XLA Modules:
  0.0 59.3 jit_solution(3577928173233962411)
XLA Ops:
  0.6 0.8 %select_reduce_fusion = f32[4,16]{1,0:T(4,128)S(1)} fusion(f32[4,8]{1,0:T(4,128)} %bitcast.53, s32[4,8]{1,0:T(4,128)} %bitcast.54), kind=kLoop, calls=%fused_computation.26 | loop fusion | flops 1472 | bytes 512 | tf_op jit(solution)/shard_map/reduce_sum | solution.py:195
  1.6 0.8 %pad_maximum_fusion.2 = bf16[4,3712]{1,0:T(4,128)(2,1)S(1)} fusion(bf16[4,128]{1,0:T(4,128)(2,1)S(1)} %fusion.22, bf16[4,3584]{1,0:T(4,128)(2,1)} %bitcast.51), kind=kLoop, calls=%fused_computation.24 | loop fusion | flops 59392 | bytes 59392 | tf_op jit(solution)/shard_map/concatenate | solution.py:200
  2.4 5.1 %collective-permute-start.2 = (bf16[4,3712]{1,0:T(4,128)(2,1)S(1)}, bf16[4,3712]{1,0:T(4,128)(2,1)S(1)}, u32[]{:S(2)}, u32[]{:S(2)}) collective-permute-start(bf16[4,3712]{1,0:T(4,128)(2,1)S(1)} %pad_maximum_fusion.2), channel_id=1, source_target_pairs={{0,24},{1,25},{2,26},{3,27},{4,28},{5,29},{6,30},{7,31},{8,16},{9,... | collective-permute-start | bytes 89096 | tf_op jit(solution)/shard_map/ppermute | solution.py:32
  7.5 0.6 %collective-permute-start = (bf16[4,3712]{1,0:T(4,128)(2,1)S(1)}, bf16[4,3712]{1,0:T(4,128)(2,1)S(1)}, u32[]{:S(2)}, u32[]{:S(2)}) collective-permute-start(bf16[4,3712]{1,0:T(4,128)(2,1)S(1)} %pad_maximum_fusion.2), channel_id=1, source_target_pairs={{0,8},{1,9},{2,10},{3,11},{4,12},{5,13},{6,14},{7,15},{8,0},{9,1},... | collective-permute-start | bytes 89096 | tf_op jit(solution)/shard_map/ppermute | solution.py:32
  8.1 1.2 %collective-permute-done.2 = bf16[4,3712]{1,0:T(4,128)(2,1)S(1)} collective-permute-done((bf16[4,3712]{1,0:T(4,128)(2,1)S(1)}, bf16[4,3712]{1,0:T(4,128)(2,1)S(1)}, u32[]{:S(2)}, u32[]{:S(2)}) %collective-permute-start.2) | collective-permute-done | bytes 29728 | tf_op jit(solution)/shard_map/ppermute | solution.py:32
  9.3 2.9 %collective-permute-done.1 = bf16[4,3712]{1,0:T(4,128)(2,1)S(1)} collective-permute-done((bf16[4,3712]{1,0:T(4,128)(2,1)S(1)}, bf16[4,3712]{1,0:T(4,128)(2,1)S(1)}, u32[]{:S(2)}, u32[]{:S(2)}) %collective-permute-start.1) | collective-permute-done | bytes 29728 | tf_op jit(solution)/shard_map/ppermute | solution.py:32
  12.2 0.8 %pad_maximum_fusion.1 = bf16[16,3712]{1,0:T(8,128)(2,1)S(1)} fusion(bf16[4,3712]{1,0:T(4,128)(2,1)S(1)} %collective-permute-done.2, bf16[4,3712]{1,0:T(4,128)(2,1)S(1)} %collective-permute-done.1, bf16[4,3712]{1,0:T(4,128)(2,1)S(1)} %collective-permute-done, bf16[4,128]{1,0:T(4,128)(2,1)S(1)} %fusion.22, bf16[4,3584]{1,0:T(4,128)(2,1)} %bitcast.52), kind=kLoop, calls=%fused_computation.22 | loop fusion | flops 593920 | bytes 237568 | tf_op jit(solution)/shard_map/concatenate | solution.py:204
  13.1 2.5 %collective-permute-start.5 = (bf16[16,3712]{1,0:T(8,128)(2,1)S(1)}, bf16[16,3712]{1,0:T(8,128)(2,1)S(1)}, u32[]{:S(2)}, u32[]{:S(2)}) collective-permute-start(bf16[16,3712]{1,0:T(8,128)(2,1)S(1)} %pad_maximum_fusion.1), channel_id=1, source_target_pairs={{0,5},{1,4},{2,7},{3,6},{4,1},{5,0},{6,3},{7,2},{8,13},{9,12},{10,... | collective-permute-start | bytes 356360 | tf_op jit(solution)/shard_map/ppermute | solution.py:32
  15.6 0.5 collective-permute-start.4
  16.1 0.5 collective-permute-start.3
  16.6 0.7 %maximum_bitcast_fusion = s32[32]{0:T(128)S(1)} fusion(s32[1,32]{1,0:T(1,128)} %param.13), kind=kLoop, calls=%fused_computation.43 | loop fusion | flops 32 | bytes 256 | tf_op jit(solution)/shard_map/max | solution.py:180
  17.3 2.9 %collective-permute-done.5 = bf16[16,3712]{1,0:T(8,128)(2,1)S(1)} collective-permute-done((bf16[16,3712]{1,0:T(8,128)(2,1)S(1)}, bf16[16,3712]{1,0:T(8,128)(2,1)S(1)}, u32[]{:S(2)}, u32[]{:S(2)}) %collective-permute-start.5) | collective-permute-done | bytes 118816 | tf_op jit(solution)/shard_map/ppermute | solution.py:32
  20.1 0.8 %collective-permute-done.4 = bf16[16,3712]{1,0:T(8,128)(2,1)S(1)} collective-permute-done((bf16[16,3712]{1,0:T(8,128)(2,1)S(1)}, bf16[16,3712]{1,0:T(8,128)(2,1)S(1)}, u32[]{:S(2)}, u32[]{:S(2)}) %collective-permute-start.4) | collective-permute-done | bytes 118816 | tf_op jit(solution)/shard_map/ppermute | solution.py:32
  21.2 1.5 %gather_fusion = bf16[32,16,576]{2,1,0:T(8,128)(2,1)} fusion(bf16[32,16,576]{2,1,0:T(8,128)(2,1)S(1)} %bitcast.46, s32[1024]{0:T(1024)S(1)} %pad_clamp_fusion.1), kind=kCustom, calls=%fused_computation | custom fusion | bytes 1179776 | tf_op jit(solution)/shard_map/gather | solution.py:180
  22.7 4.4 %all-to-all-start = ((bf16[16,2,16,576]{3,2,1,0:T(8,128)(2,1)}), bf16[16,2,16,576]{3,2,1,0:T(8,128)(2,1)S(1)}, u32[]{:S(2)}, u32[]{:S(2)}) async-start(bf16[16,2,16,576]{3,2,1,0:T(8,128)(2,1)} %bitcast.7), calls=%async_computation | async-start | bytes 1310720 | tf_op jit(solution)/shard_map/all_to_all | solution.py:181
  27.3 7.0 %experts.1 = (bf16[64,3584]{1,0:T(8,128)(2,1)S(1)}, bf16[64,3584]{1,0:T(8,128)(2,1)S(1)}) custom-call(s32[2]{0:T(128)S(1)} %pad_add_fusion.first_ref, bf16[64,3712]{1,0:T(8,128)(2,1)S(1)} %concatenate.19.own_ref, bf16[64,3712]{1,0:T(8,128)(2,1)S(1)} %collective-permute-done.6.got_ref, bf16[1,3584,512]{2,1,0:T(8,128)(2,1)} %gate_hbm.1, ...), custom_call_target="tpu_custom_call" | custom-call | flops 14092861440 | bytes 11010048 | tf_op jit(solution)/shard_map/experts/pallas_call | solution.py:117
  34.4 0.5 collective-permute-start.7
  34.9 1.4 %collective-permute-done.7 = bf16[64,3584]{1,0:T(8,128)(2,1)S(1)} collective-permute-done((bf16[64,3584]{1,0:T(8,128)(2,1)S(1)}, bf16[64,3584]{1,0:T(8,128)(2,1)S(1)}, u32[]{:S(2)}, u32[]{:S(2)}) %collective-permute-start.7) | collective-permute-done | bytes 458784 | tf_op jit(solution)/shard_map/ppermute | solution.py:32
  36.4 0.6 %collective-permute-start.8 = (bf16[16,3584]{1,0:T(8,128)(2,1)S(1)}, bf16[16,3584]{1,0:T(8,128)(2,1)S(1)}, u32[]{:S(2)}, u32[]{:S(2)}) collective-permute-start(bf16[16,3584]{1,0:T(8,128)(2,1)S(1)} %get-tuple-element.12), channel_id=1, source_target_pairs={{0,1},{1,0},{2,3},{3,2},{4,5},{5,4},{6,7},{7,6},{8,9},{9,8},{10,11... | collective-permute-start | bytes 344072 | tf_op jit(solution)/shard_map/ppermute | solution.py:32
  37.1 2.8 %collective-permute-start.10 = (bf16[16,3584]{1,0:T(8,128)(2,1)S(1)}, bf16[16,3584]{1,0:T(8,128)(2,1)S(1)}, u32[]{:S(2)}, u32[]{:S(2)}) collective-permute-start(bf16[16,3584]{1,0:T(8,128)(2,1)S(1)} %get-tuple-element.13), channel_id=1, source_target_pairs={{0,5},{1,4},{2,7},{3,6},{4,1},{5,0},{6,3},{7,2},{8,13},{9,12},{10,... | collective-permute-start | bytes 344072 | tf_op jit(solution)/shard_map/ppermute | solution.py:32
  40.1 2.4 %collective-permute-done.8 = bf16[16,3584]{1,0:T(8,128)(2,1)S(1)} collective-permute-done((bf16[16,3584]{1,0:T(8,128)(2,1)S(1)}, bf16[16,3584]{1,0:T(8,128)(2,1)S(1)}, u32[]{:S(2)}, u32[]{:S(2)}) %collective-permute-start.8) | collective-permute-done | bytes 114720 | tf_op jit(solution)/shard_map/ppermute | solution.py:32
  42.5 3.6 %collective-permute-done.10 = bf16[16,3584]{1,0:T(8,128)(2,1)S(1)} collective-permute-done((bf16[16,3584]{1,0:T(8,128)(2,1)S(1)}, bf16[16,3584]{1,0:T(8,128)(2,1)S(1)}, u32[]{:S(2)}, u32[]{:S(2)}) %collective-permute-start.10) | collective-permute-done | bytes 114720 | tf_op jit(solution)/shard_map/ppermute | solution.py:32
  46.1 2.2 %collective-permute-done.9 = bf16[16,3584]{1,0:T(8,128)(2,1)S(1)} collective-permute-done((bf16[16,3584]{1,0:T(8,128)(2,1)S(1)}, bf16[16,3584]{1,0:T(8,128)(2,1)S(1)}, u32[]{:S(2)}, u32[]{:S(2)}) %collective-permute-start.9) | collective-permute-done | bytes 114720 | tf_op jit(solution)/shard_map/ppermute | solution.py:32
  48.4 0.7 %gather_fusion.1 = bf16[32,16,576]{2,1,0:T(8,128)(2,1)S(1)} fusion(bf16[32,16,576]{2,1,0:T(8,128)(2,1)S(1)} %bitcast.47, s32[1024]{0:T(1024)S(1)} %pad_clamp_fusion), kind=kCustom, calls=%fused_computation.1 | custom fusion | bytes 1179776 | tf_op jit(solution)/shard_map/gather | solution.py:220
  49.1 0.7 %fusion.32 = f32[2,4,64]{2,1,0:T(4,128)S(1)} fusion(bf16[2,4,576]{2,1,0:T(4,128)(2,1)S(1)} %bitcast.56, bf16[1,2,4,64,576]{4,3,2,1,0:T(8,128)(2,1)S(1)} %copy-done.3, bf16[2,256,576]{2,1,0:T(8,128)(2,1)S(1)} %bitcast.48, pred[2,4,260]{2,1,0:T(4,128)(4,1)S(1)} %broadcast_or_fusion), kind=kOutput, calls=%fused_computation.52 | convolution fusion | flops 155085056 | bytes 1192992 | tf_op jit(solution)/shard_map/sub | solution.py:153
  49.9 0.6 fusion.4
  50.5 1.0 %collective-permute-start.11 = (bf16[4,3584]{1,0:T(4,128)(2,1)S(1)}, bf16[4,3584]{1,0:T(4,128)(2,1)S(1)}, u32[]{:S(2)}, u32[]{:S(2)}) collective-permute-start(bf16[4,3584]{1,0:T(4,128)(2,1)S(1)} %get-tuple-element.15), channel_id=1, source_target_pairs={{0,8},{1,9},{2,10},{3,11},{4,12},{5,13},{6,14},{7,15},{8,0},{9,1},... | collective-permute-start | bytes 86024 | tf_op jit(solution)/shard_map/ppermute | solution.py:32
  51.5 2.4 %collective-permute-start.13 = (bf16[4,3584]{1,0:T(4,128)(2,1)S(1)}, bf16[4,3584]{1,0:T(4,128)(2,1)S(1)}, u32[]{:S(2)}, u32[]{:S(2)}) collective-permute-start(bf16[4,3584]{1,0:T(4,128)(2,1)S(1)} %get-tuple-element.16), channel_id=1, source_target_pairs={{0,24},{1,25},{2,26},{3,27},{4,28},{5,29},{6,30},{7,31},{8,16},{9,... | collective-permute-start | bytes 86024 | tf_op jit(solution)/shard_map/ppermute | solution.py:32
  54.0 1.9 %fusion.5 = bf16[1,2,4,64,512]{4,3,2,1,0:T(8,128)(2,1)} fusion(bf16[2,256,576]{2,1,0:T(8,128)(2,1)S(1)} %bitcast.50, bf16[2,4,576]{2,1,0:T(4,128)(2,1)S(1)} %bitcast.58, f32[2,4,64]{2,1,0:T(4,128)S(1)} %fusion.32, f32[2,4,64,260]{3,2,1,0:T(8,128)S(1)} %fusion.4), kind=kOutput, calls=%fused_computation.9 | convolution fusion | flops 138042112 | bytes 2766848 | tf_op jit(solution)/shard_map/rshk,rkv->rshv/dot_general | solution.py:156
  56.0 1.2 %collective-permute-done.13 = bf16[4,3584]{1,0:T(4,128)(2,1)S(1)} collective-permute-done((bf16[4,3584]{1,0:T(4,128)(2,1)S(1)}, bf16[4,3584]{1,0:T(4,128)(2,1)S(1)}, u32[]{:S(2)}, u32[]{:S(2)}) %collective-permute-start.13) | collective-permute-done | bytes 28704 | tf_op jit(solution)/shard_map/ppermute | solution.py:32
  57.2 1.5 %collective-permute-done.12 = bf16[4,3584]{1,0:T(4,128)(2,1)S(1)} collective-permute-done((bf16[4,3584]{1,0:T(4,128)(2,1)S(1)}, bf16[4,3584]{1,0:T(4,128)(2,1)S(1)}, u32[]{:S(2)}, u32[]{:S(2)}) %collective-permute-start.12) | collective-permute-done | bytes 28704 | tf_op jit(solution)/shard_map/ppermute | solution.py:32
  58.6 0.6 %fusion.14 = bf16[1,4,3584]{2,1,0:T(4,128)(2,1)} fusion(bf16[4,3584]{1,0:T(4,128)(2,1)S(1)} %collective-permute-done.13, bf16[4,3584]{1,0:T(4,128)(2,1)S(1)} %collective-permute-done.12, bf16[4,3584]{1,0:T(4,128)(2,1)S(1)} %collective-permute-done.11, bf16[16,3584]{1,0:T(8,128)(2,1)S(1)} %add_convert_fusion.1), kind=kLoop, calls=%fused_computation.25 | loop fusion | flops 114688 | bytes 143360 | tf_op jit(solution)/shard_map/broadcast_in_dim | solution.py:222
  (36 shorter events, 1.2 us)
Async XLA Ops:
  0.6 20.6 %copy-start = (bf16[1,32,16,576]{3,2,1,0:T(8,128)(2,1)S(1)}, bf16[1,32,16,576]{3,2,1,0:T(8,128)(2,1)}, u32[]{:S(2)}) copy-start(bf16[1,32,16,576]{3,2,1,0:T(8,128)(2,1)} %param.12) | copy-start | bytes 1769476
  2.4 7.0 %collective-permute-start.2 = (bf16[4,3712]{1,0:T(4,128)(2,1)S(1)}, bf16[4,3712]{1,0:T(4,128)(2,1)S(1)}, u32[]{:S(2)}, u32[]{:S(2)}) collective-permute-start(bf16[4,3712]{1,0:T(4,128)(2,1)S(1)} %pad_maximum_fusion.2), channel_id=1, source_target_pairs={{0,24},{1,25},{2,26},{3,27},{4,28},{5,29},{6,30},{7,31},{8,16},{9,... | collective-permute-start | bytes 89096 | tf_op jit(solution)/shard_map/ppermute | solution.py:32
  7.5 4.8 %collective-permute-start.1 = (bf16[4,3712]{1,0:T(4,128)(2,1)S(1)}, bf16[4,3712]{1,0:T(4,128)(2,1)S(1)}, u32[]{:S(2)}, u32[]{:S(2)}) collective-permute-start(bf16[4,3712]{1,0:T(4,128)(2,1)S(1)} %pad_maximum_fusion.2), channel_id=1, source_target_pairs={{0,16},{1,17},{2,18},{3,19},{4,20},{5,21},{6,22},{7,23},{8,24},{9,... | collective-permute-start | bytes 89096 | tf_op jit(solution)/shard_map/ppermute | solution.py:32
  7.5 4.8 %collective-permute-start = (bf16[4,3712]{1,0:T(4,128)(2,1)S(1)}, bf16[4,3712]{1,0:T(4,128)(2,1)S(1)}, u32[]{:S(2)}, u32[]{:S(2)}) collective-permute-start(bf16[4,3712]{1,0:T(4,128)(2,1)S(1)} %pad_maximum_fusion.2), channel_id=1, source_target_pairs={{0,8},{1,9},{2,10},{3,11},{4,12},{5,13},{6,14},{7,15},{8,0},{9,1},... | collective-permute-start | bytes 89096 | tf_op jit(solution)/shard_map/ppermute | solution.py:32
  13.1 7.1 %collective-permute-start.5 = (bf16[16,3712]{1,0:T(8,128)(2,1)S(1)}, bf16[16,3712]{1,0:T(8,128)(2,1)S(1)}, u32[]{:S(2)}, u32[]{:S(2)}) collective-permute-start(bf16[16,3712]{1,0:T(8,128)(2,1)S(1)} %pad_maximum_fusion.1), channel_id=1, source_target_pairs={{0,5},{1,4},{2,7},{3,6},{4,1},{5,0},{6,3},{7,2},{8,13},{9,12},{10,... | collective-permute-start | bytes 356360 | tf_op jit(solution)/shard_map/ppermute | solution.py:32
  15.6 5.3 %collective-permute-start.4 = (bf16[16,3712]{1,0:T(8,128)(2,1)S(1)}, bf16[16,3712]{1,0:T(8,128)(2,1)S(1)}, u32[]{:S(2)}, u32[]{:S(2)}) collective-permute-start(bf16[16,3712]{1,0:T(8,128)(2,1)S(1)} %pad_maximum_fusion.1), channel_id=1, source_target_pairs={{0,4},{1,5},{2,6},{3,7},{4,0},{5,1},{6,2},{7,3},{8,12},{9,13},{10,... | collective-permute-start | bytes 356360 | tf_op jit(solution)/shard_map/ppermute | solution.py:32
  16.1 4.8 %collective-permute-start.3 = (bf16[16,3712]{1,0:T(8,128)(2,1)S(1)}, bf16[16,3712]{1,0:T(8,128)(2,1)S(1)}, u32[]{:S(2)}, u32[]{:S(2)}) collective-permute-start(bf16[16,3712]{1,0:T(8,128)(2,1)S(1)} %pad_maximum_fusion.1), channel_id=1, source_target_pairs={{0,1},{1,0},{2,3},{3,2},{4,5},{5,4},{6,7},{7,6},{8,9},{9,8},{10,11... | collective-permute-start | bytes 356360 | tf_op jit(solution)/shard_map/ppermute | solution.py:32
  21.1 6.1 %copy-start.2 = (s32[1,2]{1,0:T(1,128)S(1)}, s32[1,2]{1,0:T(1,128)}, u32[]{:S(2)}) copy-start(s32[1,2]{1,0:T(1,128)} %param.15) | copy-start | bytes 28
  21.1 6.2 %collective-permute-start.6 = (bf16[64,3712]{1,0:T(8,128)(2,1)S(1)}, bf16[64,3712]{1,0:T(8,128)(2,1)S(1)}, u32[]{:S(2)}, u32[]{:S(2)}) collective-permute-start(bf16[64,3712]{1,0:T(8,128)(2,1)S(1)} %concatenate.19.own_ref), channel_id=1, source_target_pairs={{0,2},{1,3},{2,0},{3,1},{4,6},{5,7},{6,4},{7,5},{8,10},{9,11},{10,... | collective-permute-start | bytes 1425416 | tf_op jit(solution)/shard_map/ppermute | solution.py:32
  22.7 25.7 %all-to-all-start = ((bf16[16,2,16,576]{3,2,1,0:T(8,128)(2,1)}), bf16[16,2,16,576]{3,2,1,0:T(8,128)(2,1)S(1)}, u32[]{:S(2)}, u32[]{:S(2)}) async-start(bf16[16,2,16,576]{3,2,1,0:T(8,128)(2,1)} %bitcast.7), calls=%async_computation | async-start | bytes 1310720 | tf_op jit(solution)/shard_map/all_to_all | solution.py:181
  34.3 5.7 %copy-start.1 = (s32[1,2,16]{2,1,0:T(2,128)S(1)}, s32[1,2,16]{2,1,0:T(2,128)}, u32[]{:S(2)}) copy-start(s32[1,2,16]{2,1,0:T(2,128)} %param.14) | copy-start | bytes 388
  34.4 1.9 %collective-permute-start.7 = (bf16[64,3584]{1,0:T(8,128)(2,1)S(1)}, bf16[64,3584]{1,0:T(8,128)(2,1)S(1)}, u32[]{:S(2)}, u32[]{:S(2)}) collective-permute-start(bf16[64,3584]{1,0:T(8,128)(2,1)S(1)} %get-tuple-element.7), channel_id=1, source_target_pairs={{0,2},{1,3},{2,0},{3,1},{4,6},{5,7},{6,4},{7,5},{8,10},{9,11},{10,... | collective-permute-start | bytes 1376264 | tf_op jit(solution)/shard_map/ppermute | solution.py:32
  36.4 12.7 %copy-start.3 = (bf16[1,2,4,64,576]{4,3,2,1,0:T(8,128)(2,1)S(1)}, bf16[1,2,4,64,576]{4,3,2,1,0:T(8,128)(2,1)}, u32[]{:S(2)}) copy-start(bf16[1,2,4,64,576]{4,3,2,1,0:T(8,128)(2,1)} %param.17) | copy-start | bytes 1769476
  36.4 12.7 %copy-start.4 = (bf16[1,2,4,576]{3,2,1,0:T(4,128)(2,1)S(1)}, bf16[1,2,4,576]{3,2,1,0:T(4,128)(2,1)}, u32[]{:S(2)}) copy-start(bf16[1,2,4,576]{3,2,1,0:T(4,128)(2,1)} %param.16) | copy-start | bytes 27652
  36.4 6.0 %collective-permute-start.8 = (bf16[16,3584]{1,0:T(8,128)(2,1)S(1)}, bf16[16,3584]{1,0:T(8,128)(2,1)S(1)}, u32[]{:S(2)}, u32[]{:S(2)}) collective-permute-start(bf16[16,3584]{1,0:T(8,128)(2,1)S(1)} %get-tuple-element.12), channel_id=1, source_target_pairs={{0,1},{1,0},{2,3},{3,2},{4,5},{5,4},{6,7},{7,6},{8,9},{9,8},{10,11... | collective-permute-start | bytes 344072 | tf_op jit(solution)/shard_map/ppermute | solution.py:32
  37.1 9.1 %collective-permute-start.10 = (bf16[16,3584]{1,0:T(8,128)(2,1)S(1)}, bf16[16,3584]{1,0:T(8,128)(2,1)S(1)}, u32[]{:S(2)}, u32[]{:S(2)}) collective-permute-start(bf16[16,3584]{1,0:T(8,128)(2,1)S(1)} %get-tuple-element.13), channel_id=1, source_target_pairs={{0,5},{1,4},{2,7},{3,6},{4,1},{5,0},{6,3},{7,2},{8,13},{9,12},{10,... | collective-permute-start | bytes 344072 | tf_op jit(solution)/shard_map/ppermute | solution.py:32
  39.9 8.5 %collective-permute-start.9 = (bf16[16,3584]{1,0:T(8,128)(2,1)S(1)}, bf16[16,3584]{1,0:T(8,128)(2,1)S(1)}, u32[]{:S(2)}, u32[]{:S(2)}) collective-permute-start(bf16[16,3584]{1,0:T(8,128)(2,1)S(1)} %get-tuple-element.14), channel_id=1, source_target_pairs={{0,4},{1,5},{2,6},{3,7},{4,0},{5,1},{6,2},{7,3},{8,12},{9,13},{10,... | collective-permute-start | bytes 344072 | tf_op jit(solution)/shard_map/ppermute | solution.py:32
  50.5 5.5 %collective-permute-start.11 = (bf16[4,3584]{1,0:T(4,128)(2,1)S(1)}, bf16[4,3584]{1,0:T(4,128)(2,1)S(1)}, u32[]{:S(2)}, u32[]{:S(2)}) collective-permute-start(bf16[4,3584]{1,0:T(4,128)(2,1)S(1)} %get-tuple-element.15), channel_id=1, source_target_pairs={{0,8},{1,9},{2,10},{3,11},{4,12},{5,13},{6,14},{7,15},{8,0},{9,1},... | collective-permute-start | bytes 86024 | tf_op jit(solution)/shard_map/ppermute | solution.py:32
  51.5 5.7 %collective-permute-start.13 = (bf16[4,3584]{1,0:T(4,128)(2,1)S(1)}, bf16[4,3584]{1,0:T(4,128)(2,1)S(1)}, u32[]{:S(2)}, u32[]{:S(2)}) collective-permute-start(bf16[4,3584]{1,0:T(4,128)(2,1)S(1)} %get-tuple-element.16), channel_id=1, source_target_pairs={{0,24},{1,25},{2,26},{3,27},{4,28},{5,29},{6,30},{7,31},{8,16},{9,... | collective-permute-start | bytes 86024 | tf_op jit(solution)/shard_map/ppermute | solution.py:32
  53.8 4.8 %collective-permute-start.12 = (bf16[4,3584]{1,0:T(4,128)(2,1)S(1)}, bf16[4,3584]{1,0:T(4,128)(2,1)S(1)}, u32[]{:S(2)}, u32[]{:S(2)}) collective-permute-start(bf16[4,3584]{1,0:T(4,128)(2,1)S(1)} %get-tuple-element.17), channel_id=1, source_target_pairs={{0,16},{1,17},{2,18},{3,19},{4,20},{5,21},{6,22},{7,23},{8,24},{9,... | collective-permute-start | bytes 86024 | tf_op jit(solution)/shard_map/ppermute | solution.py:32

commit v2 on v1

--- a/solution.py
+++ b/solution.py
@@ -66,13 +66,18 @@
         part = (own, slice(None), pl.ds(turn * wide, wide))
         return pltpu.make_async_copy(down_hbm.at[part], down_ref.at[part], down_sem.at[own, turn])
 
-    for own in range(owned):
-        for turn in range(turns):
-            load_in(0, own, turn).start()
-            load_in(1, own, turn).start()
-    for turn in range(ends):
-        for own in range(owned):
-            load_down(own, turn).start()
+    order = [(own, turn) for own in range(owned) for turn in range(turns)]
+
+    def load_next(at):
+        if at < len(order):
+            load_in(0, *order[at]).start()
+            load_in(1, *order[at]).start()
+        elif at == len(order):
+            for turn in range(ends):
+                for own in range(owned):
+                    load_down(own, turn).start()
+
+    load_next(0)
     rows_ref[:count] = own_ref[...]
     rows_ref[count:] = got_ref[...]
     extra = rows_ref[:, width:].astype(jnp.float32)
@@ -86,6 +91,7 @@
             part = pl.ds(turn * step, step)
             x = rows_ref[:, :width]
             load_in(0, own, turn).wait()
+            load_next(order.index((own, turn)) + 1)
             gate = jnp.dot(x, gate_ref[own, :, part], preferred_element_type=jnp.float32)
             load_in(1, own, turn).wait()
             up = jnp.dot(x, up_ref[own, :, part], preferred_element_type=jnp.float32)
@@ -199,9 +205,10 @@
     pad = -extra.shape[1] % 128
     packed = jnp.concatenate([moe_rows[0], jnp.pad(extra, ((0, 0), (0, pad)))], axis=1)
     far, near, last = levels_of(peers, lax.axis_size(("section", "tp")))
-    pooled = packed
+    pooled = packed[None]
     for bits in pairs_of(far):
         pooled = jnp.concatenate([pooled] + [exchange(pooled, mask) for mask in masks_of(bits)[1:]], axis=0)
+    pooled = pooled.reshape(-1, packed.shape[1])
     pooled = jnp.concatenate([pooled] + [exchange(pooled, mask) for mask in masks_of(near)[1:]], axis=0)
     other = masks_of(last)[-1]
     first = lax.axis_index("dev") * owned

time: 59.6 us -> 58.5 us (0.982)
  other arithmetic: 4.18 us -> 3.48 us
    broadcast_in_dim x0 -> x1, other arithmetic: none -> 0.76 us  [body(): pooled = packed[None]]
    concatenate x1 -> x0, other arithmetic: 0.76 us -> none  [body(): jnp.concatenate([moe_rows[0], jnp.pad(extra, ((0, 0), (0, pad)))], axis=1)]
    concatenate x1, other arithmetic: 0.82 us -> 0.1 us  [body(): jnp.concatenate([pooled] + [exchange(pooled, mask) for mask in masks_of(b...]
    max x1, other arithmetic: 0.01 us -> 0.68 us  [body(): jnp.maximum(table, 0)]
    max x1, other arithmetic: 0.66 us -> 0.01 us  [body(): picked_pages = pages[jnp.maximum(outgoing_slots, 0)]]
  transfers between devices with their start and end apart: 15 -> 15, of which waited for: 10 -> 9; matrix products, arithmetic and copies ran while one was open for 8% -> 8% of each run, Pallas kernels for 12% -> 11%
where the time goes in v2:
time: 58.5 us; the launch traced here: 58.2 us
  starting transfers between devices  21.4 us (37%)
  waiting for transfers between devices  20.1 us (34%)
  Pallas kernels  6.68 us (11%)
  other arithmetic  3.48 us (6%)
  matrix products  3.25 us (6%)
  local copies, waits for them, and re-layouts  2.41 us (4%)
  between operations  0.84 us (1%)
    ppermute x14, waiting for transfers between devices, exchange(): return lax.ppermute(value, RANK, [(at, at ^ mask) for at in range(count)])  20.1 us
    ppermute x14, starting transfers between devices, exchange(): return lax.ppermute(value, RANK, [(at, at ^ mask) for at in range(count)])  17 us
    pallas_call x1, Pallas kernels, experts_of(): pl.pallas_call(experts_kernel, out_shape=(half, half), in_specs=[pl.Block...  6.68 us
    all_to_all x1, starting transfers between devices, body(): lax.all_to_all(picked_pages.reshape(peers, capp, page_len, width_lat), 'd...  4.44 us
    dot_general x1, matrix products, attend(): jnp.einsum('rshk,rkv->rshv', weights, values, preferred_element_type=jnp....  1.94 us
    gather x1, local copies, waits for them, and re-layouts, body(): picked_pages = pages[jnp.maximum(outgoing_slots, 0)]  1.48 us
  transfers between devices with their start and end apart: 15, of which 9 were waited for; matrix products, arithmetic and copies ran while one was open for 8% of the time, Pallas kernels for 11%

profile of v2, /device:TPU:0, one launch (start us, length us, event | category | flops | bytes accessed | tf_op | source)
XLA Modules:
  0.0 58.2 jit_solution(3866754151237795872)
XLA Ops:
  0.7 0.9 %select_reduce_fusion = f32[4,16]{1,0:T(4,128)S(1)} fusion(f32[4,8]{1,0:T(4,128)} %bitcast.54, s32[4,8]{1,0:T(4,128)} %bitcast.55), kind=kLoop, calls=%fused_computation.26 | loop fusion | flops 1472 | bytes 512 | tf_op jit(solution)/shard_map/reduce_sum | solution.py:201
  1.6 0.8 %maximum_bitcast_fusion = bf16[1,4,3712]{2,1,0:T(4,128)(2,1)S(1)} fusion(bf16[4,128]{1,0:T(4,128)(2,1)S(1)} %fusion.22, bf16[4,3584]{1,0:T(4,128)(2,1)} %bitcast.53), kind=kLoop, calls=%fused_computation.24 | loop fusion | flops 59392 | bytes 59392 | tf_op jit(solution)/shard_map/broadcast_in_dim | solution.py:208
  2.4 5.1 %collective-permute-start.2 = (bf16[1,4,3712]{2,1,0:T(4,128)(2,1)S(1)}, bf16[1,4,3712]{2,1,0:T(4,128)(2,1)S(1)}, u32[]{:S(2)}, u32[]{:S(2)}) collective-permute-start(bf16[1,4,3712]{2,1,0:T(4,128)(2,1)S(1)} %maximum_bitcast_fusion), channel_id=1, source_target_pairs={{0,24},{1,25},{2,26},{3,27},{4,28},{5,29},{6,30},{7,31},{8,16},{9,... | collective-permute-start | bytes 89096 | tf_op jit(solution)/shard_map/ppermute | solution.py:32
  7.5 0.6 %collective-permute-start = (bf16[1,4,3712]{2,1,0:T(4,128)(2,1)S(1)}, bf16[1,4,3712]{2,1,0:T(4,128)(2,1)S(1)}, u32[]{:S(2)}, u32[]{:S(2)}) collective-permute-start(bf16[1,4,3712]{2,1,0:T(4,128)(2,1)S(1)} %maximum_bitcast_fusion), channel_id=1, source_target_pairs={{0,8},{1,9},{2,10},{3,11},{4,12},{5,13},{6,14},{7,15},{8,0},{9,1},... | collective-permute-start | bytes 89096 | tf_op jit(solution)/shard_map/ppermute | solution.py:32
  8.1 0.7 %broadcast_maximum_fusion = s32[1,2,16]{2,1,0:T(2,128)S(1)} fusion(s32[1,2,16]{2,1,0:T(2,128)} %param.14), kind=kLoop, calls=%fused_computation.46 | loop fusion | flops 32 | bytes 256 | tf_op jit(solution)/shard_map/max | solution.py:227
  8.9 0.5 collective-permute-done.2
  9.3 2.9 %collective-permute-done.1 = bf16[1,4,3712]{2,1,0:T(4,128)(2,1)S(1)} collective-permute-done((bf16[1,4,3712]{2,1,0:T(4,128)(2,1)S(1)}, bf16[1,4,3712]{2,1,0:T(4,128)(2,1)S(1)}, u32[]{:S(2)}, u32[]{:S(2)}) %collective-permute-start.1) | collective-permute-done | bytes 29728 | tf_op jit(solution)/shard_map/ppermute | solution.py:32
  12.4 2.5 %collective-permute-start.5 = (bf16[16,3712]{1,0:T(8,128)(2,1)S(1)}, bf16[16,3712]{1,0:T(8,128)(2,1)S(1)}, u32[]{:S(2)}, u32[]{:S(2)}) collective-permute-start(bf16[16,3712]{1,0:T(8,128)(2,1)S(1)} %reshape.110), channel_id=1, source_target_pairs={{0,5},{1,4},{2,7},{3,6},{4,1},{5,0},{6,3},{7,2},{8,13},{9,12},{10,... | collective-permute-start | bytes 356360 | tf_op jit(solution)/shard_map/ppermute | solution.py:32
  14.9 0.5 collective-permute-start.4
  15.4 0.5 collective-permute-start.3
  16.0 4.3 %collective-permute-done.3 = bf16[16,3712]{1,0:T(8,128)(2,1)S(1)} collective-permute-done((bf16[16,3712]{1,0:T(8,128)(2,1)S(1)}, bf16[16,3712]{1,0:T(8,128)(2,1)S(1)}, u32[]{:S(2)}, u32[]{:S(2)}) %collective-permute-start.3) | collective-permute-done | bytes 118816 | tf_op jit(solution)/shard_map/ppermute | solution.py:32
  20.5 1.5 %gather_fusion = bf16[32,16,576]{2,1,0:T(8,128)(2,1)} fusion(bf16[32,16,576]{2,1,0:T(8,128)(2,1)S(1)} %bitcast.48, s32[1024]{0:T(1024)S(1)} %get-tuple-element.19), kind=kCustom, calls=%fused_computation | custom fusion | bytes 1179776 | tf_op jit(solution)/shard_map/gather | solution.py:186
  21.9 4.4 %all-to-all-start = ((bf16[16,2,16,576]{3,2,1,0:T(8,128)(2,1)}), bf16[16,2,16,576]{3,2,1,0:T(8,128)(2,1)S(1)}, u32[]{:S(2)}, u32[]{:S(2)}) async-start(bf16[16,2,16,576]{3,2,1,0:T(8,128)(2,1)} %bitcast.8), calls=%async_computation | async-start | bytes 1310720 | tf_op jit(solution)/shard_map/all_to_all | solution.py:187
  26.5 6.7 %experts.1 = (bf16[64,3584]{1,0:T(8,128)(2,1)S(1)}, bf16[64,3584]{1,0:T(8,128)(2,1)S(1)}) custom-call(s32[2]{0:T(128)S(1)} %pad_add_fusion.first_ref, bf16[64,3712]{1,0:T(8,128)(2,1)S(1)} %constant_dynamic-update-slice_fusion.own_ref, bf16[64,3712]{1,0:T(8,128)(2,1)S(1)} %collective-permute-done.6.got_ref, bf16[1,3584,512]{2,1,0:T(8,128)(2,1)} %gate_hbm.1, ...), custom_call_target="tpu_custom_call" | custom-call | flops 14092861440 | bytes 11010048 | tf_op jit(solution)/shard_map/experts/pallas_call | solution.py:123
  33.2 0.5 collective-permute-start.7
  33.7 1.4 %collective-permute-done.7 = bf16[64,3584]{1,0:T(8,128)(2,1)S(1)} collective-permute-done((bf16[64,3584]{1,0:T(8,128)(2,1)S(1)}, bf16[64,3584]{1,0:T(8,128)(2,1)S(1)}, u32[]{:S(2)}, u32[]{:S(2)}) %collective-permute-start.7) | collective-permute-done | bytes 458784 | tf_op jit(solution)/shard_map/ppermute | solution.py:32
  35.3 0.6 %collective-permute-start.8 = (bf16[16,3584]{1,0:T(8,128)(2,1)S(1)}, bf16[16,3584]{1,0:T(8,128)(2,1)S(1)}, u32[]{:S(2)}, u32[]{:S(2)}) collective-permute-start(bf16[16,3584]{1,0:T(8,128)(2,1)S(1)} %get-tuple-element.12), channel_id=1, source_target_pairs={{0,1},{1,0},{2,3},{3,2},{4,5},{5,4},{6,7},{7,6},{8,9},{9,8},{10,11... | collective-permute-start | bytes 344072 | tf_op jit(solution)/shard_map/ppermute | solution.py:32
  35.9 2.8 %collective-permute-start.10 = (bf16[16,3584]{1,0:T(8,128)(2,1)S(1)}, bf16[16,3584]{1,0:T(8,128)(2,1)S(1)}, u32[]{:S(2)}, u32[]{:S(2)}) collective-permute-start(bf16[16,3584]{1,0:T(8,128)(2,1)S(1)} %get-tuple-element.13), channel_id=1, source_target_pairs={{0,5},{1,4},{2,7},{3,6},{4,1},{5,0},{6,3},{7,2},{8,13},{9,12},{10,... | collective-permute-start | bytes 344072 | tf_op jit(solution)/shard_map/ppermute | solution.py:32
  38.7 0.2 collective-permute-start.9
  38.8 2.5 %collective-permute-done.8 = bf16[16,3584]{1,0:T(8,128)(2,1)S(1)} collective-permute-done((bf16[16,3584]{1,0:T(8,128)(2,1)S(1)}, bf16[16,3584]{1,0:T(8,128)(2,1)S(1)}, u32[]{:S(2)}, u32[]{:S(2)}) %collective-permute-start.8) | collective-permute-done | bytes 114720 | tf_op jit(solution)/shard_map/ppermute | solution.py:32
  41.3 3.8 %collective-permute-done.10 = bf16[16,3584]{1,0:T(8,128)(2,1)S(1)} collective-permute-done((bf16[16,3584]{1,0:T(8,128)(2,1)S(1)}, bf16[16,3584]{1,0:T(8,128)(2,1)S(1)}, u32[]{:S(2)}, u32[]{:S(2)}) %collective-permute-start.10) | collective-permute-done | bytes 114720 | tf_op jit(solution)/shard_map/ppermute | solution.py:32
  45.1 2.2 %collective-permute-done.9 = bf16[16,3584]{1,0:T(8,128)(2,1)S(1)} collective-permute-done((bf16[16,3584]{1,0:T(8,128)(2,1)S(1)}, bf16[16,3584]{1,0:T(8,128)(2,1)S(1)}, u32[]{:S(2)}, u32[]{:S(2)}) %collective-permute-start.9) | collective-permute-done | bytes 114720 | tf_op jit(solution)/shard_map/ppermute | solution.py:32
  47.4 0.7 %gather_fusion.1 = bf16[32,16,576]{2,1,0:T(8,128)(2,1)S(1)} fusion(bf16[32,16,576]{2,1,0:T(8,128)(2,1)S(1)} %bitcast.49, s32[1024]{0:T(1024)S(1)} %get-tuple-element.18), kind=kCustom, calls=%fused_computation.1 | custom fusion | bytes 1179776 | tf_op jit(solution)/shard_map/gather | solution.py:227
  48.1 0.7 %fusion.32 = f32[2,4,64]{2,1,0:T(4,128)S(1)} fusion(bf16[2,4,576]{2,1,0:T(4,128)(2,1)S(1)} %bitcast.57, bf16[1,2,4,64,576]{4,3,2,1,0:T(8,128)(2,1)S(1)} %copy-done.2, bf16[2,256,576]{2,1,0:T(8,128)(2,1)S(1)} %bitcast.50, pred[2,4,260]{2,1,0:T(4,128)(4,1)S(1)} %broadcast_or_fusion), kind=kOutput, calls=%fused_computation.56 | convolution fusion | flops 155085056 | bytes 1192992 | tf_op jit(solution)/shard_map/sub | solution.py:159
  48.9 0.6 fusion.4
  49.5 0.8 %collective-permute-start.11 = (bf16[4,3584]{1,0:T(4,128)(2,1)S(1)}, bf16[4,3584]{1,0:T(4,128)(2,1)S(1)}, u32[]{:S(2)}, u32[]{:S(2)}) collective-permute-start(bf16[4,3584]{1,0:T(4,128)(2,1)S(1)} %get-tuple-element.15), channel_id=1, source_target_pairs={{0,8},{1,9},{2,10},{3,11},{4,12},{5,13},{6,14},{7,15},{8,0},{9,1},... | collective-permute-start | bytes 86024 | tf_op jit(solution)/shard_map/ppermute | solution.py:32
  50.3 2.4 %collective-permute-start.13 = (bf16[4,3584]{1,0:T(4,128)(2,1)S(1)}, bf16[4,3584]{1,0:T(4,128)(2,1)S(1)}, u32[]{:S(2)}, u32[]{:S(2)}) collective-permute-start(bf16[4,3584]{1,0:T(4,128)(2,1)S(1)} %get-tuple-element.16), channel_id=1, source_target_pairs={{0,24},{1,25},{2,26},{3,27},{4,28},{5,29},{6,30},{7,31},{8,16},{9,... | collective-permute-start | bytes 86024 | tf_op jit(solution)/shard_map/ppermute | solution.py:32
  52.7 0.4 collective-permute-start.12
  53.0 1.9 %fusion.5 = bf16[1,2,4,64,512]{4,3,2,1,0:T(8,128)(2,1)} fusion(bf16[2,256,576]{2,1,0:T(8,128)(2,1)S(1)} %bitcast.52, bf16[2,4,576]{2,1,0:T(4,128)(2,1)S(1)} %bitcast.59, f32[2,4,64]{2,1,0:T(4,128)S(1)} %fusion.32, f32[2,4,64,260]{3,2,1,0:T(8,128)S(1)} %fusion.4), kind=kOutput, calls=%fused_computation.9 | convolution fusion | flops 138042112 | bytes 2766848 | tf_op jit(solution)/shard_map/rshk,rkv->rshv/dot_general | solution.py:162
  55.0 1.0 %collective-permute-done.13 = bf16[4,3584]{1,0:T(4,128)(2,1)S(1)} collective-permute-done((bf16[4,3584]{1,0:T(4,128)(2,1)S(1)}, bf16[4,3584]{1,0:T(4,128)(2,1)S(1)}, u32[]{:S(2)}, u32[]{:S(2)}) %collective-permute-start.13) | collective-permute-done | bytes 28704 | tf_op jit(solution)/shard_map/ppermute | solution.py:32
  56.0 1.5 %collective-permute-done.12 = bf16[4,3584]{1,0:T(4,128)(2,1)S(1)} collective-permute-done((bf16[4,3584]{1,0:T(4,128)(2,1)S(1)}, bf16[4,3584]{1,0:T(4,128)(2,1)S(1)}, u32[]{:S(2)}, u32[]{:S(2)}) %collective-permute-start.12) | collective-permute-done | bytes 28704 | tf_op jit(solution)/shard_map/ppermute | solution.py:32
  57.5 0.6 %fusion.14 = bf16[1,4,3584]{2,1,0:T(4,128)(2,1)} fusion(bf16[4,3584]{1,0:T(4,128)(2,1)S(1)} %collective-permute-done.13, bf16[4,3584]{1,0:T(4,128)(2,1)S(1)} %collective-permute-done.12, bf16[4,3584]{1,0:T(4,128)(2,1)S(1)} %collective-permute-done.11, bf16[16,3584]{1,0:T(8,128)(2,1)S(1)} %add_convert_fusion.1), kind=kLoop, calls=%fused_computation.25 | loop fusion | flops 114688 | bytes 143360 | tf_op jit(solution)/shard_map/broadcast_in_dim | solution.py:229
  (39 shorter events, 0.9 us)
Async XLA Ops:
  0.6 19.8 %copy-start = (bf16[1,32,16,576]{3,2,1,0:T(8,128)(2,1)S(1)}, bf16[1,32,16,576]{3,2,1,0:T(8,128)(2,1)}, u32[]{:S(2)}) copy-start(bf16[1,32,16,576]{3,2,1,0:T(8,128)(2,1)} %param.12) | copy-start | bytes 1769476
  0.6 19.8 %copy-start.4 = (s32[1,32]{1,0:T(1,128)S(1)}, s32[1,32]{1,0:T(1,128)}, u32[]{:S(2)}) copy-start(s32[1,32]{1,0:T(1,128)} %param.13) | copy-start | bytes 388
  2.4 7.0 %collective-permute-start.2 = (bf16[1,4,3712]{2,1,0:T(4,128)(2,1)S(1)}, bf16[1,4,3712]{2,1,0:T(4,128)(2,1)S(1)}, u32[]{:S(2)}, u32[]{:S(2)}) collective-permute-start(bf16[1,4,3712]{2,1,0:T(4,128)(2,1)S(1)} %maximum_bitcast_fusion), channel_id=1, source_target_pairs={{0,24},{1,25},{2,26},{3,27},{4,28},{5,29},{6,30},{7,31},{8,16},{9,... | collective-permute-start | bytes 89096 | tf_op jit(solution)/shard_map/ppermute | solution.py:32
  7.5 4.8 %collective-permute-start.1 = (bf16[1,4,3712]{2,1,0:T(4,128)(2,1)S(1)}, bf16[1,4,3712]{2,1,0:T(4,128)(2,1)S(1)}, u32[]{:S(2)}, u32[]{:S(2)}) collective-permute-start(bf16[1,4,3712]{2,1,0:T(4,128)(2,1)S(1)} %maximum_bitcast_fusion), channel_id=1, source_target_pairs={{0,16},{1,17},{2,18},{3,19},{4,20},{5,21},{6,22},{7,23},{8,24},{9,... | collective-permute-start | bytes 89096 | tf_op jit(solution)/shard_map/ppermute | solution.py:32
  7.5 4.8 %collective-permute-start = (bf16[1,4,3712]{2,1,0:T(4,128)(2,1)S(1)}, bf16[1,4,3712]{2,1,0:T(4,128)(2,1)S(1)}, u32[]{:S(2)}, u32[]{:S(2)}) collective-permute-start(bf16[1,4,3712]{2,1,0:T(4,128)(2,1)S(1)} %maximum_bitcast_fusion), channel_id=1, source_target_pairs={{0,8},{1,9},{2,10},{3,11},{4,12},{5,13},{6,14},{7,15},{8,0},{9,1},... | collective-permute-start | bytes 89096 | tf_op jit(solution)/shard_map/ppermute | solution.py:32
  12.4 7.9 %collective-permute-start.5 = (bf16[16,3712]{1,0:T(8,128)(2,1)S(1)}, bf16[16,3712]{1,0:T(8,128)(2,1)S(1)}, u32[]{:S(2)}, u32[]{:S(2)}) collective-permute-start(bf16[16,3712]{1,0:T(8,128)(2,1)S(1)} %reshape.110), channel_id=1, source_target_pairs={{0,5},{1,4},{2,7},{3,6},{4,1},{5,0},{6,3},{7,2},{8,13},{9,12},{10,... | collective-permute-start | bytes 356360 | tf_op jit(solution)/shard_map/ppermute | solution.py:32
  14.9 5.4 %collective-permute-start.4 = (bf16[16,3712]{1,0:T(8,128)(2,1)S(1)}, bf16[16,3712]{1,0:T(8,128)(2,1)S(1)}, u32[]{:S(2)}, u32[]{:S(2)}) collective-permute-start(bf16[16,3712]{1,0:T(8,128)(2,1)S(1)} %reshape.110), channel_id=1, source_target_pairs={{0,4},{1,5},{2,6},{3,7},{4,0},{5,1},{6,2},{7,3},{8,12},{9,13},{10,... | collective-permute-start | bytes 356360 | tf_op jit(solution)/shard_map/ppermute | solution.py:32
  15.4 4.8 %collective-permute-start.3 = (bf16[16,3712]{1,0:T(8,128)(2,1)S(1)}, bf16[16,3712]{1,0:T(8,128)(2,1)S(1)}, u32[]{:S(2)}, u32[]{:S(2)}) collective-permute-start(bf16[16,3712]{1,0:T(8,128)(2,1)S(1)} %reshape.110), channel_id=1, source_target_pairs={{0,1},{1,0},{2,3},{3,2},{4,5},{5,4},{6,7},{7,6},{8,9},{9,8},{10,11... | collective-permute-start | bytes 356360 | tf_op jit(solution)/shard_map/ppermute | solution.py:32
  20.3 6.1 %collective-permute-start.6 = (bf16[64,3712]{1,0:T(8,128)(2,1)S(1)}, bf16[64,3712]{1,0:T(8,128)(2,1)S(1)}, u32[]{:S(2)}, u32[]{:S(2)}) collective-permute-start(bf16[64,3712]{1,0:T(8,128)(2,1)S(1)} %constant_dynamic-update-slice_fusion.own_ref), channel_id=1, source_target_pairs={{0,2},{1,3},{2,0},{3,1},{4,6},{5,7},{6,4},{7,5},{8,10},{9,11},{10,... | collective-permute-start | bytes 1425416 | tf_op jit(solution)/shard_map/ppermute | solution.py:32
  21.9 25.5 %all-to-all-start = ((bf16[16,2,16,576]{3,2,1,0:T(8,128)(2,1)}), bf16[16,2,16,576]{3,2,1,0:T(8,128)(2,1)S(1)}, u32[]{:S(2)}, u32[]{:S(2)}) async-start(bf16[16,2,16,576]{3,2,1,0:T(8,128)(2,1)} %bitcast.8), calls=%async_computation | async-start | bytes 1310720 | tf_op jit(solution)/shard_map/all_to_all | solution.py:187
  26.5 7.2 %copy-start.1 = (s32[1,2]{1,0:T(1,128)S(1)}, s32[1,2]{1,0:T(1,128)}, u32[]{:S(2)}) copy-start(s32[1,2]{1,0:T(1,128)} %param.15) | copy-start | bytes 28
  33.2 1.9 %collective-permute-start.7 = (bf16[64,3584]{1,0:T(8,128)(2,1)S(1)}, bf16[64,3584]{1,0:T(8,128)(2,1)S(1)}, u32[]{:S(2)}, u32[]{:S(2)}) collective-permute-start(bf16[64,3584]{1,0:T(8,128)(2,1)S(1)} %get-tuple-element.7), channel_id=1, source_target_pairs={{0,2},{1,3},{2,0},{3,1},{4,6},{5,7},{6,4},{7,5},{8,10},{9,11},{10,... | collective-permute-start | bytes 1376264 | tf_op jit(solution)/shard_map/ppermute | solution.py:32
  35.2 12.9 %copy-start.2 = (bf16[1,2,4,64,576]{4,3,2,1,0:T(8,128)(2,1)S(1)}, bf16[1,2,4,64,576]{4,3,2,1,0:T(8,128)(2,1)}, u32[]{:S(2)}) copy-start(bf16[1,2,4,64,576]{4,3,2,1,0:T(8,128)(2,1)} %param.17) | copy-start | bytes 1769476
  35.2 12.9 %copy-start.3 = (bf16[1,2,4,576]{3,2,1,0:T(4,128)(2,1)S(1)}, bf16[1,2,4,576]{3,2,1,0:T(4,128)(2,1)}, u32[]{:S(2)}) copy-start(bf16[1,2,4,576]{3,2,1,0:T(4,128)(2,1)} %param.16) | copy-start | bytes 27652
  35.3 6.0 %collective-permute-start.8 = (bf16[16,3584]{1,0:T(8,128)(2,1)S(1)}, bf16[16,3584]{1,0:T(8,128)(2,1)S(1)}, u32[]{:S(2)}, u32[]{:S(2)}) collective-permute-start(bf16[16,3584]{1,0:T(8,128)(2,1)S(1)} %get-tuple-element.12), channel_id=1, source_target_pairs={{0,1},{1,0},{2,3},{3,2},{4,5},{5,4},{6,7},{7,6},{8,9},{9,8},{10,11... | collective-permute-start | bytes 344072 | tf_op jit(solution)/shard_map/ppermute | solution.py:32
  35.9 9.3 %collective-permute-start.10 = (bf16[16,3584]{1,0:T(8,128)(2,1)S(1)}, bf16[16,3584]{1,0:T(8,128)(2,1)S(1)}, u32[]{:S(2)}, u32[]{:S(2)}) collective-permute-start(bf16[16,3584]{1,0:T(8,128)(2,1)S(1)} %get-tuple-element.13), channel_id=1, source_target_pairs={{0,5},{1,4},{2,7},{3,6},{4,1},{5,0},{6,3},{7,2},{8,13},{9,12},{10,... | collective-permute-start | bytes 344072 | tf_op jit(solution)/shard_map/ppermute | solution.py:32
  38.7 8.7 %collective-permute-start.9 = (bf16[16,3584]{1,0:T(8,128)(2,1)S(1)}, bf16[16,3584]{1,0:T(8,128)(2,1)S(1)}, u32[]{:S(2)}, u32[]{:S(2)}) collective-permute-start(bf16[16,3584]{1,0:T(8,128)(2,1)S(1)} %get-tuple-element.14), channel_id=1, source_target_pairs={{0,4},{1,5},{2,6},{3,7},{4,0},{5,1},{6,2},{7,3},{8,12},{9,13},{10,... | collective-permute-start | bytes 344072 | tf_op jit(solution)/shard_map/ppermute | solution.py:32
  49.5 5.5 %collective-permute-start.11 = (bf16[4,3584]{1,0:T(4,128)(2,1)S(1)}, bf16[4,3584]{1,0:T(4,128)(2,1)S(1)}, u32[]{:S(2)}, u32[]{:S(2)}) collective-permute-start(bf16[4,3584]{1,0:T(4,128)(2,1)S(1)} %get-tuple-element.15), channel_id=1, source_target_pairs={{0,8},{1,9},{2,10},{3,11},{4,12},{5,13},{6,14},{7,15},{8,0},{9,1},... | collective-permute-start | bytes 86024 | tf_op jit(solution)/shard_map/ppermute | solution.py:32
  50.3 5.7 %collective-permute-start.13 = (bf16[4,3584]{1,0:T(4,128)(2,1)S(1)}, bf16[4,3584]{1,0:T(4,128)(2,1)S(1)}, u32[]{:S(2)}, u32[]{:S(2)}) collective-permute-start(bf16[4,3584]{1,0:T(4,128)(2,1)S(1)} %get-tuple-element.16), channel_id=1, source_target_pairs={{0,24},{1,25},{2,26},{3,27},{4,28},{5,29},{6,30},{7,31},{8,16},{9,... | collective-permute-start | bytes 86024 | tf_op jit(solution)/shard_map/ppermute | solution.py:32
  52.7 4.9 %collective-permute-start.12 = (bf16[4,3584]{1,0:T(4,128)(2,1)S(1)}, bf16[4,3584]{1,0:T(4,128)(2,1)S(1)}, u32[]{:S(2)}, u32[]{:S(2)}) collective-permute-start(bf16[4,3584]{1,0:T(4,128)(2,1)S(1)} %get-tuple-element.17), channel_id=1, source_target_pairs={{0,16},{1,17},{2,18},{3,19},{4,20},{5,21},{6,22},{7,23},{8,24},{9,... | collective-permute-start | bytes 86024 | tf_op jit(solution)/shard_map/ppermute | solution.py:32

commit v3 on v2

--- a/solution.py
+++ b/solution.py
@@ -217,8 +217,14 @@
     )
     mixed = kept.astype(jnp.float32) + exchange(sent, other).astype(jnp.float32)
     mixed = mixed.astype(jnp.bfloat16)
-    mixed = collect(mixed, near)
-    mixed, arrived = lax.optimization_barrier((mixed, arrived))
+    masks = masks_of(near)
+    mixed = mixed.reshape(len(masks), -1, width)
+    got = [exchange(mixed[turn], masks[turn]) for turn in range(1, len(masks))]
+    got[0], arrived = lax.optimization_barrier((got[0], arrived))
+    total = mixed[0].astype(jnp.float32)
+    for part in got:
+        total = total + part.astype(jnp.float32)
+    mixed = total.astype(jnp.bfloat16)
     for bits in pairs_of(far)[::-1]:
         mixed = collect(mixed, bits)
 

time: 58.5 us -> 59.2 us (1.012)
  matrix products: 3.25 us -> 6.67 us
  waiting for transfers between devices: 20.1 us -> 17.2 us
    ppermute x14, waiting for transfers between devices: 20.1 us -> 12.5 us  [exchange(): return lax.ppermute(value, RANK, [(at, at ^ mask) for at in range(count)])]
    all_to_all x1, waiting for transfers between devices: 0.01 us -> 4.76 us  [body(): lax.all_to_all(picked_pages.reshape(peers, capp, page_len, width_lat), 'd...]
    dot_general x1, matrix products: 0.56 us -> 2.62 us  [attend(): jnp.einsum('rshl,rkl->rshk', queries, keys, preferred_element_type=jnp.fl...]
    dot_general x1, matrix products: 1.94 us -> 3.3 us  [attend(): jnp.einsum('rshk,rkv->rshv', weights, values, preferred_element_type=jnp....]
    ppermute x14, starting transfers between devices: 17 us -> 18 us  [exchange(): return lax.ppermute(value, RANK, [(at, at ^ mask) for at in range(count)])]
    all_to_all x1, starting transfers between devices: 4.44 us -> 3.59 us  [body(): lax.all_to_all(picked_pages.reshape(peers, capp, page_len, width_lat), 'd...]
  transfers between devices with their start and end apart: 15 -> 15, of which waited for: 9 -> 8; matrix products, arithmetic and copies ran while one was open for 8% -> 17% of each run, Pallas kernels for 11% -> 11%
where the time goes in v3:
time: 59.2 us; the launch traced here: 58.8 us
  starting transfers between devices  21.5 us (36%)
  waiting for transfers between devices  17.2 us (29%)
  Pallas kernels  6.69 us (11%)
  matrix products  6.67 us (11%)
  other arithmetic  3.48 us (6%)
  local copies, waits for them, and re-layouts  2.4 us (4%)
  between operations  0.82 us (1%)
    ppermute x14, starting transfers between devices, exchange(): return lax.ppermute(value, RANK, [(at, at ^ mask) for at in range(count)])  18 us
    ppermute x14, waiting for transfers between devices, exchange(): return lax.ppermute(value, RANK, [(at, at ^ mask) for at in range(count)])  12.5 us
    pallas_call x1, Pallas kernels, experts_of(): pl.pallas_call(experts_kernel, out_shape=(half, half), in_specs=[pl.Block...  6.69 us
    all_to_all x1, waiting for transfers between devices, body(): lax.all_to_all(picked_pages.reshape(peers, capp, page_len, width_lat), 'd...  4.76 us
    all_to_all x1, starting transfers between devices, body(): lax.all_to_all(picked_pages.reshape(peers, capp, page_len, width_lat), 'd...  3.59 us
    dot_general x1, matrix products, attend(): jnp.einsum('rshk,rkv->rshv', weights, values, preferred_element_type=jnp....  3.3 us
    dot_general x1, matrix products, attend(): jnp.einsum('rshl,rkl->rshk', queries, keys, preferred_element_type=jnp.fl...  2.62 us
    gather x1, local copies, waits for them, and re-layouts, body(): picked_pages = pages[jnp.maximum(outgoing_slots, 0)]  1.48 us
  transfers between devices with their start and end apart: 15, of which 8 were waited for; matrix products, arithmetic and copies ran while one was open for 17% of the time, Pallas kernels for 11%

profile of v3, /device:TPU:0, one launch (start us, length us, event | category | flops | bytes accessed | tf_op | source)
XLA Modules:
  0.0 58.8 jit_solution(8841750400572954103)
XLA Ops:
  0.7 0.9 %select_reduce_fusion = f32[4,16]{1,0:T(4,128)S(1)} fusion(f32[4,8]{1,0:T(4,128)} %bitcast.54, s32[4,8]{1,0:T(4,128)} %bitcast.55), kind=kLoop, calls=%fused_computation.26 | loop fusion | flops 1472 | bytes 512 | tf_op jit(solution)/shard_map/reduce_sum | solution.py:201
  1.6 0.8 %maximum_bitcast_fusion = bf16[1,4,3712]{2,1,0:T(4,128)(2,1)S(1)} fusion(bf16[4,128]{1,0:T(4,128)(2,1)S(1)} %fusion.22, bf16[4,3584]{1,0:T(4,128)(2,1)} %bitcast.53), kind=kLoop, calls=%fused_computation.24 | loop fusion | flops 59392 | bytes 59392 | tf_op jit(solution)/shard_map/broadcast_in_dim | solution.py:208
  2.4 3.1 %collective-permute-start = (bf16[1,4,3712]{2,1,0:T(4,128)(2,1)S(1)}, bf16[1,4,3712]{2,1,0:T(4,128)(2,1)S(1)}, u32[]{:S(2)}, u32[]{:S(2)}) collective-permute-start(bf16[1,4,3712]{2,1,0:T(4,128)(2,1)S(1)} %maximum_bitcast_fusion), channel_id=1, source_target_pairs={{0,8},{1,9},{2,10},{3,11},{4,12},{5,13},{6,14},{7,15},{8,0},{9,1},... | collective-permute-start | bytes 89096 | tf_op jit(solution)/shard_map/ppermute | solution.py:32
  5.5 2.6 %collective-permute-start.1 = (bf16[1,4,3712]{2,1,0:T(4,128)(2,1)S(1)}, bf16[1,4,3712]{2,1,0:T(4,128)(2,1)S(1)}, u32[]{:S(2)}, u32[]{:S(2)}) collective-permute-start(bf16[1,4,3712]{2,1,0:T(4,128)(2,1)S(1)} %maximum_bitcast_fusion), channel_id=1, source_target_pairs={{0,16},{1,17},{2,18},{3,19},{4,20},{5,21},{6,22},{7,23},{8,24},{9,... | collective-permute-start | bytes 89096 | tf_op jit(solution)/shard_map/ppermute | solution.py:32
  8.0 0.7 %broadcast_maximum_fusion = s32[1,2,16]{2,1,0:T(2,128)S(1)} fusion(s32[1,2,16]{2,1,0:T(2,128)} %param.14), kind=kLoop, calls=%fused_computation.46 | loop fusion | flops 32 | bytes 256 | tf_op jit(solution)/shard_map/max | solution.py:233
  8.8 1.9 %collective-permute-done.1 = bf16[1,4,3712]{2,1,0:T(4,128)(2,1)S(1)} collective-permute-done((bf16[1,4,3712]{2,1,0:T(4,128)(2,1)S(1)}, bf16[1,4,3712]{2,1,0:T(4,128)(2,1)S(1)}, u32[]{:S(2)}, u32[]{:S(2)}) %collective-permute-start.1) | collective-permute-done | bytes 29728 | tf_op jit(solution)/shard_map/ppermute | solution.py:32
  10.7 3.0 %collective-permute-done.2 = bf16[1,4,3712]{2,1,0:T(4,128)(2,1)S(1)} collective-permute-done((bf16[1,4,3712]{2,1,0:T(4,128)(2,1)S(1)}, bf16[1,4,3712]{2,1,0:T(4,128)(2,1)S(1)}, u32[]{:S(2)}, u32[]{:S(2)}) %collective-permute-start.2) | collective-permute-done | bytes 29728 | tf_op jit(solution)/shard_map/ppermute | solution.py:32
  13.9 1.6 %collective-permute-start.3 = (bf16[16,3712]{1,0:T(8,128)(2,1)S(1)}, bf16[16,3712]{1,0:T(8,128)(2,1)S(1)}, u32[]{:S(2)}, u32[]{:S(2)}) collective-permute-start(bf16[16,3712]{1,0:T(8,128)(2,1)S(1)} %reshape.119), channel_id=1, source_target_pairs={{0,1},{1,0},{2,3},{3,2},{4,5},{5,4},{6,7},{7,6},{8,9},{9,8},{10,11... | collective-permute-start | bytes 356360 | tf_op jit(solution)/shard_map/ppermute | solution.py:32
  15.4 1.6 %collective-permute-start.4 = (bf16[16,3712]{1,0:T(8,128)(2,1)S(1)}, bf16[16,3712]{1,0:T(8,128)(2,1)S(1)}, u32[]{:S(2)}, u32[]{:S(2)}) collective-permute-start(bf16[16,3712]{1,0:T(8,128)(2,1)S(1)} %reshape.119), channel_id=1, source_target_pairs={{0,4},{1,5},{2,6},{3,7},{4,0},{5,1},{6,2},{7,3},{8,12},{9,13},{10,... | collective-permute-start | bytes 356360 | tf_op jit(solution)/shard_map/ppermute | solution.py:32
  17.0 0.5 collective-permute-start.5
  17.5 2.3 %collective-permute-done.3 = bf16[16,3712]{1,0:T(8,128)(2,1)S(1)} collective-permute-done((bf16[16,3712]{1,0:T(8,128)(2,1)S(1)}, bf16[16,3712]{1,0:T(8,128)(2,1)S(1)}, u32[]{:S(2)}, u32[]{:S(2)}) %collective-permute-start.3) | collective-permute-done | bytes 118816 | tf_op jit(solution)/shard_map/ppermute | solution.py:32
  19.8 1.2 %collective-permute-done.4 = bf16[16,3712]{1,0:T(8,128)(2,1)S(1)} collective-permute-done((bf16[16,3712]{1,0:T(8,128)(2,1)S(1)}, bf16[16,3712]{1,0:T(8,128)(2,1)S(1)}, u32[]{:S(2)}, u32[]{:S(2)}) %collective-permute-start.4) | collective-permute-done | bytes 118816 | tf_op jit(solution)/shard_map/ppermute | solution.py:32
  21.0 1.7 %collective-permute-done.5 = bf16[16,3712]{1,0:T(8,128)(2,1)S(1)} collective-permute-done((bf16[16,3712]{1,0:T(8,128)(2,1)S(1)}, bf16[16,3712]{1,0:T(8,128)(2,1)S(1)}, u32[]{:S(2)}, u32[]{:S(2)}) %collective-permute-start.5) | collective-permute-done | bytes 118816 | tf_op jit(solution)/shard_map/ppermute | solution.py:32
  22.9 1.5 %gather_fusion = bf16[32,16,576]{2,1,0:T(8,128)(2,1)} fusion(bf16[32,16,576]{2,1,0:T(8,128)(2,1)S(1)} %bitcast.48, s32[1024]{0:T(1024)S(1)} %get-tuple-element.19), kind=kCustom, calls=%fused_computation | custom fusion | bytes 1179776 | tf_op jit(solution)/shard_map/gather | solution.py:186
  24.4 3.6 %all-to-all-start = ((bf16[16,2,16,576]{3,2,1,0:T(8,128)(2,1)}), bf16[16,2,16,576]{3,2,1,0:T(8,128)(2,1)S(1)}, u32[]{:S(2)}, u32[]{:S(2)}) async-start(bf16[16,2,16,576]{3,2,1,0:T(8,128)(2,1)} %bitcast.8), calls=%async_computation | async-start | bytes 1310720 | tf_op jit(solution)/shard_map/all_to_all | solution.py:187
  28.1 6.7 %experts.1 = (bf16[64,3584]{1,0:T(8,128)(2,1)S(1)}, bf16[64,3584]{1,0:T(8,128)(2,1)S(1)}) custom-call(s32[2]{0:T(128)S(1)} %pad_add_fusion.first_ref, bf16[64,3712]{1,0:T(8,128)(2,1)S(1)} %constant_dynamic-update-slice_fusion.own_ref, bf16[64,3712]{1,0:T(8,128)(2,1)S(1)} %collective-permute-done.6.got_ref, bf16[1,3584,512]{2,1,0:T(8,128)(2,1)} %gate_hbm.1, ...), custom_call_target="tpu_custom_call" | custom-call | flops 14092861440 | bytes 11010048 | tf_op jit(solution)/shard_map/experts/pallas_call | solution.py:123
  34.8 0.4 collective-permute-start.7
  35.3 1.4 %collective-permute-done.7 = bf16[64,3584]{1,0:T(8,128)(2,1)S(1)} collective-permute-done((bf16[64,3584]{1,0:T(8,128)(2,1)S(1)}, bf16[64,3584]{1,0:T(8,128)(2,1)S(1)}, u32[]{:S(2)}, u32[]{:S(2)}) %collective-permute-start.7) | collective-permute-done | bytes 458784 | tf_op jit(solution)/shard_map/ppermute | solution.py:32
  36.6 0.1 add_convert_fusion
  36.8 0.6 %collective-permute-start.8 = (bf16[16,3584]{1,0:T(8,128)(2,1)S(1)}, bf16[16,3584]{1,0:T(8,128)(2,1)S(1)}, u32[]{:S(2)}, u32[]{:S(2)}) collective-permute-start(bf16[16,3584]{1,0:T(8,128)(2,1)S(1)} %get-tuple-element.14), channel_id=1, source_target_pairs={{0,1},{1,0},{2,3},{3,2},{4,5},{5,4},{6,7},{7,6},{8,9},{9,8},{10,11... | collective-permute-start | bytes 344072 | tf_op jit(solution)/shard_map/ppermute | solution.py:32
  37.4 2.8 %collective-permute-start.10 = (bf16[16,3584]{1,0:T(8,128)(2,1)S(1)}, bf16[16,3584]{1,0:T(8,128)(2,1)S(1)}, u32[]{:S(2)}, u32[]{:S(2)}) collective-permute-start(bf16[16,3584]{1,0:T(8,128)(2,1)S(1)} %get-tuple-element.13), channel_id=1, source_target_pairs={{0,5},{1,4},{2,7},{3,6},{4,1},{5,0},{6,3},{7,2},{8,13},{9,12},{10,... | collective-permute-start | bytes 344072 | tf_op jit(solution)/shard_map/ppermute | solution.py:32
  40.2 0.2 collective-permute-start.9
  40.4 4.8 %all-to-all-done = bf16[16,2,16,576]{3,2,1,0:T(8,128)(2,1)S(1)} async-done(((bf16[16,2,16,576]{3,2,1,0:T(8,128)(2,1)}), bf16[16,2,16,576]{3,2,1,0:T(8,128)(2,1)S(1)}, u32[]{:S(2)}, u32[]{:S(2)}) %all-to-all-start) | async-done | bytes 589856 | tf_op jit(solution)/shard_map/all_to_all | solution.py:187
  45.2 0.7 %gather_fusion.1 = bf16[32,16,576]{2,1,0:T(8,128)(2,1)S(1)} fusion(bf16[32,16,576]{2,1,0:T(8,128)(2,1)S(1)} %bitcast.49, s32[1024]{0:T(1024)S(1)} %get-tuple-element.18), kind=kCustom, calls=%fused_computation.1 | custom fusion | bytes 1179776 | tf_op jit(solution)/shard_map/gather | solution.py:233
  45.9 2.6 %fusion.4 = f32[2,4,64,260]{3,2,1,0:T(8,128)} fusion(bf16[2,4,576]{2,1,0:T(4,128)(2,1)S(1)} %bitcast.57, bf16[1,2,4,64,576]{4,3,2,1,0:T(8,128)(2,1)} %param.17, bf16[2,256,576]{2,1,0:T(8,128)(2,1)S(1)} %bitcast.50, pred[2,4,260]{2,1,0:T(4,128)(4,1)S(1)} %broadcast_or_fusion), kind=kOutput, calls=%fused_computation.8 | convolution fusion | flops 154818560 | bytes 1723424 | tf_op jit(solution)/shard_map/rshl,rkl->rshk/dot_general | solution.py:151
  48.5 0.7 %fusion.32 = f32[2,4,64]{2,1,0:T(4,128)S(1)} fusion(bf16[2,4,576]{2,1,0:T(4,128)(2,1)S(1)} %bitcast.58, bf16[1,2,4,64,576]{4,3,2,1,0:T(8,128)(2,1)S(1)} %copy-done.2, bf16[2,256,576]{2,1,0:T(8,128)(2,1)S(1)} %bitcast.51, pred[2,4,260]{2,1,0:T(4,128)(4,1)S(1)} %broadcast_or_fusion), kind=kOutput, calls=%fused_computation.56 | convolution fusion | flops 155085056 | bytes 1192992 | tf_op jit(solution)/shard_map/sub | solution.py:159
  49.4 1.4 %collective-permute-start.11 = (bf16[4,3584]{1,0:T(4,128)(2,1)S(1)}, bf16[4,3584]{1,0:T(4,128)(2,1)S(1)}, u32[]{:S(2)}, u32[]{:S(2)}) collective-permute-start(bf16[4,3584]{1,0:T(4,128)(2,1)S(1)} %get-tuple-element.15), channel_id=1, source_target_pairs={{0,8},{1,9},{2,10},{3,11},{4,12},{5,13},{6,14},{7,15},{8,0},{9,1},... | collective-permute-start | bytes 86024 | tf_op jit(solution)/shard_map/ppermute | solution.py:32
  50.8 1.7 %collective-permute-start.12 = (bf16[4,3584]{1,0:T(4,128)(2,1)S(1)}, bf16[4,3584]{1,0:T(4,128)(2,1)S(1)}, u32[]{:S(2)}, u32[]{:S(2)}) collective-permute-start(bf16[4,3584]{1,0:T(4,128)(2,1)S(1)} %get-tuple-element.17), channel_id=1, source_target_pairs={{0,16},{1,17},{2,18},{3,19},{4,20},{5,21},{6,22},{7,23},{8,24},{9,... | collective-permute-start | bytes 86024 | tf_op jit(solution)/shard_map/ppermute | solution.py:32
  52.5 1.4 %collective-permute-start.13 = (bf16[4,3584]{1,0:T(4,128)(2,1)S(1)}, bf16[4,3584]{1,0:T(4,128)(2,1)S(1)}, u32[]{:S(2)}, u32[]{:S(2)}) collective-permute-start(bf16[4,3584]{1,0:T(4,128)(2,1)S(1)} %get-tuple-element.16), channel_id=1, source_target_pairs={{0,24},{1,25},{2,26},{3,27},{4,28},{5,29},{6,30},{7,31},{8,16},{9,... | collective-permute-start | bytes 86024 | tf_op jit(solution)/shard_map/ppermute | solution.py:32
  53.9 3.3 %fusion.5 = bf16[1,2,4,64,512]{4,3,2,1,0:T(8,128)(2,1)} fusion(bf16[2,256,576]{2,1,0:T(8,128)(2,1)S(1)} %bitcast.52, bf16[2,4,576]{2,1,0:T(4,128)(2,1)S(1)} %bitcast.59, f32[2,4,64]{2,1,0:T(4,128)S(1)} %fusion.32, f32[2,4,64,260]{3,2,1,0:T(8,128)} %fusion.4), kind=kOutput, calls=%fused_computation.9 | convolution fusion | flops 138042112 | bytes 2698240 | tf_op jit(solution)/shard_map/rshk,rkv->rshv/dot_general | solution.py:162
  57.2 1.0 %collective-permute-done.13 = bf16[4,3584]{1,0:T(4,128)(2,1)S(1)} collective-permute-done((bf16[4,3584]{1,0:T(4,128)(2,1)S(1)}, bf16[4,3584]{1,0:T(4,128)(2,1)S(1)}, u32[]{:S(2)}, u32[]{:S(2)}) %collective-permute-start.13) | collective-permute-done | bytes 28704 | tf_op jit(solution)/shard_map/ppermute | solution.py:32
  58.2 0.6 %fusion.14 = bf16[1,4,3584]{2,1,0:T(4,128)(2,1)} fusion(bf16[4,3584]{1,0:T(4,128)(2,1)S(1)} %collective-permute-done.13, bf16[4,3584]{1,0:T(4,128)(2,1)S(1)} %collective-permute-done.12, bf16[4,3584]{1,0:T(4,128)(2,1)S(1)} %collective-permute-done.11, bf16[16,3584]{1,0:T(8,128)(2,1)S(1)} %add_convert_fusion.1), kind=kLoop, calls=%fused_computation.25 | loop fusion | flops 114688 | bytes 143360 | tf_op jit(solution)/shard_map/broadcast_in_dim | solution.py:235
  (39 shorter events, 0.8 us)
Async XLA Ops:
  0.6 22.3 %copy-start = (bf16[1,32,16,576]{3,2,1,0:T(8,128)(2,1)S(1)}, bf16[1,32,16,576]{3,2,1,0:T(8,128)(2,1)}, u32[]{:S(2)}) copy-start(bf16[1,32,16,576]{3,2,1,0:T(8,128)(2,1)} %param.12) | copy-start | bytes 1769476
  0.6 22.2 %copy-start.4 = (s32[1,32]{1,0:T(1,128)S(1)}, s32[1,32]{1,0:T(1,128)}, u32[]{:S(2)}) copy-start(s32[1,32]{1,0:T(1,128)} %param.13) | copy-start | bytes 388
  2.4 6.5 %collective-permute-start = (bf16[1,4,3712]{2,1,0:T(4,128)(2,1)S(1)}, bf16[1,4,3712]{2,1,0:T(4,128)(2,1)S(1)}, u32[]{:S(2)}, u32[]{:S(2)}) collective-permute-start(bf16[1,4,3712]{2,1,0:T(4,128)(2,1)S(1)} %maximum_bitcast_fusion), channel_id=1, source_target_pairs={{0,8},{1,9},{2,10},{3,11},{4,12},{5,13},{6,14},{7,15},{8,0},{9,1},... | collective-permute-start | bytes 89096 | tf_op jit(solution)/shard_map/ppermute | solution.py:32
  5.5 5.3 %collective-permute-start.1 = (bf16[1,4,3712]{2,1,0:T(4,128)(2,1)S(1)}, bf16[1,4,3712]{2,1,0:T(4,128)(2,1)S(1)}, u32[]{:S(2)}, u32[]{:S(2)}) collective-permute-start(bf16[1,4,3712]{2,1,0:T(4,128)(2,1)S(1)} %maximum_bitcast_fusion), channel_id=1, source_target_pairs={{0,16},{1,17},{2,18},{3,19},{4,20},{5,21},{6,22},{7,23},{8,24},{9,... | collective-permute-start | bytes 89096 | tf_op jit(solution)/shard_map/ppermute | solution.py:32
  8.0 5.7 %collective-permute-start.2 = (bf16[1,4,3712]{2,1,0:T(4,128)(2,1)S(1)}, bf16[1,4,3712]{2,1,0:T(4,128)(2,1)S(1)}, u32[]{:S(2)}, u32[]{:S(2)}) collective-permute-start(bf16[1,4,3712]{2,1,0:T(4,128)(2,1)S(1)} %maximum_bitcast_fusion), channel_id=1, source_target_pairs={{0,24},{1,25},{2,26},{3,27},{4,28},{5,29},{6,30},{7,31},{8,16},{9,... | collective-permute-start | bytes 89096 | tf_op jit(solution)/shard_map/ppermute | solution.py:32
  13.9 5.9 %collective-permute-start.3 = (bf16[16,3712]{1,0:T(8,128)(2,1)S(1)}, bf16[16,3712]{1,0:T(8,128)(2,1)S(1)}, u32[]{:S(2)}, u32[]{:S(2)}) collective-permute-start(bf16[16,3712]{1,0:T(8,128)(2,1)S(1)} %reshape.119), channel_id=1, source_target_pairs={{0,1},{1,0},{2,3},{3,2},{4,5},{5,4},{6,7},{7,6},{8,9},{9,8},{10,11... | collective-permute-start | bytes 356360 | tf_op jit(solution)/shard_map/ppermute | solution.py:32
  15.4 5.6 %collective-permute-start.4 = (bf16[16,3712]{1,0:T(8,128)(2,1)S(1)}, bf16[16,3712]{1,0:T(8,128)(2,1)S(1)}, u32[]{:S(2)}, u32[]{:S(2)}) collective-permute-start(bf16[16,3712]{1,0:T(8,128)(2,1)S(1)} %reshape.119), channel_id=1, source_target_pairs={{0,4},{1,5},{2,6},{3,7},{4,0},{5,1},{6,2},{7,3},{8,12},{9,13},{10,... | collective-permute-start | bytes 356360 | tf_op jit(solution)/shard_map/ppermute | solution.py:32
  17.0 5.7 %collective-permute-start.5 = (bf16[16,3712]{1,0:T(8,128)(2,1)S(1)}, bf16[16,3712]{1,0:T(8,128)(2,1)S(1)}, u32[]{:S(2)}, u32[]{:S(2)}) collective-permute-start(bf16[16,3712]{1,0:T(8,128)(2,1)S(1)} %reshape.119), channel_id=1, source_target_pairs={{0,5},{1,4},{2,7},{3,6},{4,1},{5,0},{6,3},{7,2},{8,13},{9,12},{10,... | collective-permute-start | bytes 356360 | tf_op jit(solution)/shard_map/ppermute | solution.py:32
  22.8 5.3 %collective-permute-start.6 = (bf16[64,3712]{1,0:T(8,128)(2,1)S(1)}, bf16[64,3712]{1,0:T(8,128)(2,1)S(1)}, u32[]{:S(2)}, u32[]{:S(2)}) collective-permute-start(bf16[64,3712]{1,0:T(8,128)(2,1)S(1)} %constant_dynamic-update-slice_fusion.own_ref), channel_id=1, source_target_pairs={{0,2},{1,3},{2,0},{3,1},{4,6},{5,7},{6,4},{7,5},{8,10},{9,11},{10,... | collective-permute-start | bytes 1425416 | tf_op jit(solution)/shard_map/ppermute | solution.py:32
  24.4 20.8 %all-to-all-start = ((bf16[16,2,16,576]{3,2,1,0:T(8,128)(2,1)}), bf16[16,2,16,576]{3,2,1,0:T(8,128)(2,1)S(1)}, u32[]{:S(2)}, u32[]{:S(2)}) async-start(bf16[16,2,16,576]{3,2,1,0:T(8,128)(2,1)} %bitcast.8), calls=%async_computation | async-start | bytes 1310720 | tf_op jit(solution)/shard_map/all_to_all | solution.py:187
  28.1 7.1 %copy-start.1 = (s32[1,2]{1,0:T(1,128)S(1)}, s32[1,2]{1,0:T(1,128)}, u32[]{:S(2)}) copy-start(s32[1,2]{1,0:T(1,128)} %param.15) | copy-start | bytes 28
  34.8 1.9 %collective-permute-start.7 = (bf16[64,3584]{1,0:T(8,128)(2,1)S(1)}, bf16[64,3584]{1,0:T(8,128)(2,1)S(1)}, u32[]{:S(2)}, u32[]{:S(2)}) collective-permute-start(bf16[64,3584]{1,0:T(8,128)(2,1)S(1)} %get-tuple-element.7), channel_id=1, source_target_pairs={{0,2},{1,3},{2,0},{3,1},{4,6},{5,7},{6,4},{7,5},{8,10},{9,11},{10,... | collective-permute-start | bytes 1376264 | tf_op jit(solution)/shard_map/ppermute | solution.py:32
  36.7 9.1 %copy-start.3 = (bf16[1,2,4,576]{3,2,1,0:T(4,128)(2,1)S(1)}, bf16[1,2,4,576]{3,2,1,0:T(4,128)(2,1)}, u32[]{:S(2)}) copy-start(bf16[1,2,4,576]{3,2,1,0:T(4,128)(2,1)} %param.16) | copy-start | bytes 27652
  36.8 8.4 %collective-permute-start.8 = (bf16[16,3584]{1,0:T(8,128)(2,1)S(1)}, bf16[16,3584]{1,0:T(8,128)(2,1)S(1)}, u32[]{:S(2)}, u32[]{:S(2)}) collective-permute-start(bf16[16,3584]{1,0:T(8,128)(2,1)S(1)} %get-tuple-element.14), channel_id=1, source_target_pairs={{0,1},{1,0},{2,3},{3,2},{4,5},{5,4},{6,7},{7,6},{8,9},{9,8},{10,11... | collective-permute-start | bytes 344072 | tf_op jit(solution)/shard_map/ppermute | solution.py:32
  37.4 11.8 %collective-permute-start.10 = (bf16[16,3584]{1,0:T(8,128)(2,1)S(1)}, bf16[16,3584]{1,0:T(8,128)(2,1)S(1)}, u32[]{:S(2)}, u32[]{:S(2)}) collective-permute-start(bf16[16,3584]{1,0:T(8,128)(2,1)S(1)} %get-tuple-element.13), channel_id=1, source_target_pairs={{0,5},{1,4},{2,7},{3,6},{4,1},{5,0},{6,3},{7,2},{8,13},{9,12},{10,... | collective-permute-start | bytes 344072 | tf_op jit(solution)/shard_map/ppermute | solution.py:32
  40.2 9.1 %collective-permute-start.9 = (bf16[16,3584]{1,0:T(8,128)(2,1)S(1)}, bf16[16,3584]{1,0:T(8,128)(2,1)S(1)}, u32[]{:S(2)}, u32[]{:S(2)}) collective-permute-start(bf16[16,3584]{1,0:T(8,128)(2,1)S(1)} %get-tuple-element.12), channel_id=1, source_target_pairs={{0,4},{1,5},{2,6},{3,7},{4,0},{5,1},{6,2},{7,3},{8,12},{9,13},{10,... | collective-permute-start | bytes 344072 | tf_op jit(solution)/shard_map/ppermute | solution.py:32
  45.9 2.6 %copy-start.2 = (bf16[1,2,4,64,576]{4,3,2,1,0:T(8,128)(2,1)S(1)}, bf16[1,2,4,64,576]{4,3,2,1,0:T(8,128)(2,1)}, u32[]{:S(2)}) copy-start(bf16[1,2,4,64,576]{4,3,2,1,0:T(8,128)(2,1)} %param.17) | copy-start | bytes 1769476
  49.4 7.8 %collective-permute-start.11 = (bf16[4,3584]{1,0:T(4,128)(2,1)S(1)}, bf16[4,3584]{1,0:T(4,128)(2,1)S(1)}, u32[]{:S(2)}, u32[]{:S(2)}) collective-permute-start(bf16[4,3584]{1,0:T(4,128)(2,1)S(1)} %get-tuple-element.15), channel_id=1, source_target_pairs={{0,8},{1,9},{2,10},{3,11},{4,12},{5,13},{6,14},{7,15},{8,0},{9,1},... | collective-permute-start | bytes 86024 | tf_op jit(solution)/shard_map/ppermute | solution.py:32
  50.8 6.4 %collective-permute-start.12 = (bf16[4,3584]{1,0:T(4,128)(2,1)S(1)}, bf16[4,3584]{1,0:T(4,128)(2,1)S(1)}, u32[]{:S(2)}, u32[]{:S(2)}) collective-permute-start(bf16[4,3584]{1,0:T(4,128)(2,1)S(1)} %get-tuple-element.17), channel_id=1, source_target_pairs={{0,16},{1,17},{2,18},{3,19},{4,20},{5,21},{6,22},{7,23},{8,24},{9,... | collective-permute-start | bytes 86024 | tf_op jit(solution)/shard_map/ppermute | solution.py:32
  52.5 5.7 %collective-permute-start.13 = (bf16[4,3584]{1,0:T(4,128)(2,1)S(1)}, bf16[4,3584]{1,0:T(4,128)(2,1)S(1)}, u32[]{:S(2)}, u32[]{:S(2)}) collective-permute-start(bf16[4,3584]{1,0:T(4,128)(2,1)S(1)} %get-tuple-element.16), channel_id=1, source_target_pairs={{0,24},{1,25},{2,26},{3,27},{4,28},{5,29},{6,30},{7,31},{8,16},{9,... | collective-permute-start | bytes 86024 | tf_op jit(solution)/shard_map/ppermute | solution.py:32
